TPU v7x, 256 devices: a whole 4x4x8 slice. The times are simulated.
256 devices in a mesh: tile: 32 (over x_hi, z, core), row: 8 (over y, x_lo).
Axes of the slice: x: 4 (x_hi: 2, x_lo: 2; x = x_hi * 2 + x_lo), y: 4, z: 8, core: 2. Of those that a mesh axis runs over, the one named last changes fastest.
Arguments:
- activations: bfloat16 [96, 48, 48, 256], P('tile', 'row'), may hold values from -6 to 6
- matching: int32 [96, 4, 4], replicated, may hold values from 0 to 95, as said below
- first_kernel_weight: bfloat16 [3, 3, 256, 256], replicated, may hold values from -0.125 to 0.125
- conv_second: bfloat16 [3, 3, 256, 256], replicated, may hold values from -0.125 to 0.125
- reduce_kernel_weight: bfloat16 [2, 2, 256, 256], replicated, may hold values from -0.1875 to 0.1875
- cotangent: bfloat16 [96, 24, 24, 256], P('tile', 'row'), may hold values from -6 to 6
Outputs:
- output: bfloat16 [96, 24, 24, 256], P('tile', 'row')
- grad_activations: bfloat16 [96, 48, 48, 256], P('tile', 'row')
- first_kernel_gradient: float32 [3, 3, 256, 256], replicated
- grad_conv_second: float32 [3, 3, 256, 256], replicated
- grad_down: float32 [2, 2, 256, 256], replicated
Inputs may be any that keep to these rules, and one draw needn't show every extreme that they name: Entry [t, s] (s = 0 top, 1 bottom, 2 left, 3 right) holds a neighbour tile n, its side s2, a reversal flag f of 0 or 1 and a count q of quarter turns, 0 to 3. The list is a matching of all 384 tile sides: entry [n, s2] holds t, s, the same f and (4 - q) % 4, and no side is matched with itself.
All inputs are finite; a program needn't handle non-finite values.
Results may differ from a plain program's by a relative error of at most 0.013.
Values may be sent and summed in bfloat16 or wider, within the bound.
No kernel may reach another device: no remote copies, remote signals or barrier semaphores. Data moves between devices by JAX's collectives and lax.ppermute only.
A program may use at most 128 MiB of HBM per device.

v0:
```python
import functools
import math

import jax
import jax.numpy as jnp
import numpy as np
from jax import lax
from jax.experimental import pallas as pl
from jax.experimental.pallas import tpu as pltpu
from jax.sharding import Mesh, PartitionSpec as P

XH, Z, CORE, Y, XL = 2, 8, 2, 4, 2
ROWS = Y * XL
UNITS = 2
EXTRA = 14
TILE_AXES = ("xh", "z", "c")
ROW_AXES = ("y", "xl")
COLUMN_AXES = ("xh", "c")
f32 = jnp.float32
bf16 = jnp.bfloat16


def broadcast_all(piece, axes, count):
    return lax.all_to_all(
        jnp.broadcast_to(piece[None], (count,) + piece.shape), axes, 0, 0, tiled=True
    )


def column_of(group):
    return (group // (Z * CORE)) * CORE + group % CORE


def routing(matching, strip, channels):
    tiles = matching.shape[0]
    here = tiles // (XH * Z * CORE)
    lines = here * 4
    xh, z, core = lax.axis_index("xh"), lax.axis_index("z"), lax.axis_index("c")
    me = xh * CORE + core
    sides = matching.reshape(tiles * 4, 4)
    grouped = matching.reshape(XH, Z, CORE, lines, 4)
    column = lax.dynamic_index_in_dim(grouped, z, 1, keepdims=False).reshape(XH * CORE * lines, 4)
    tile, side = column[:, 0], column[:, 1]
    beside = jnp.where(side < 2, 2, 0)[:, None] + jnp.arange(2)[None, :]
    corners = sides[tile[:, None] * 4 + beside]
    finish = (side[:, None] % 2) ^ corners[..., 2]

    row = lax.axis_index(ROW_AXES)
    cells = UNITS * strip
    piece = cells * lines
    width = ROWS * strip

    def place(tile, side):
        group = tile // here
        held = column_of(group) == me
        return held, ((group // CORE) % Z) * piece + (tile % here) * 4 + side

    def own(table):
        return lax.dynamic_slice_in_dim(table, me * lines, lines, 0)

    held, at = place(tile, side)
    columns = XH * CORE
    cell = np.arange(cells, dtype=np.int32)[None, :, None] * lines
    pick = jnp.where(held.reshape(columns, 1, lines), at.reshape(columns, 1, lines) + cell, -1)
    held, at = place(corners[..., 0], corners[..., 1])
    at = jnp.where(held, at, -Z * piece).reshape(columns, lines, 2).swapaxes(1, 2)
    depth = np.array([0, 1, 0, 1], np.int32)
    depth = jnp.where(row == 0, depth, strip - 1 - depth)[None, :, None] * lines
    pick = jnp.concatenate([pick, jnp.repeat(at, 2, axis=1) + depth], axis=1).reshape(-1)

    mine, my_corners = own(column), own(corners)
    sent = piece + 4 * lines
    source = column_of(mine[:, 0] // here)[None, :]
    source_corner = column_of(my_corners[..., 0] // here).T
    select = jnp.concatenate(
        [jnp.broadcast_to(source, (cells, lines)), jnp.repeat(source_corner, 2, axis=0)], axis=0
    ).reshape(-1) * sent + np.arange(sent, dtype=np.int32)

    flipped = jnp.broadcast_to(mine[:, 2:3] == 1, (lines, width)).reshape(-1)
    position = np.arange(width, dtype=np.int32)[None, :]
    line = np.arange(lines, dtype=np.int32)[:, None]
    count = lines * width

    def places(position, step, base):
        return (position * step + line * base).reshape(-1)

    kind = jnp.broadcast_to(mine[:, 1:2], (lines, width)).reshape(-1)
    kind = (kind[None, :, None] == np.arange(4, dtype=np.int32)[:, None, None]).astype(bf16)
    kind = jnp.broadcast_to(kind, (4, count, channels))
    ends = jnp.repeat(own(finish).T, 2, axis=0)
    turned = jnp.where(
        flipped, places(width - 1 - position, lines, 1), places(position, lines, 1)
    )
    flip = jnp.where(flipped, places(width - 1 - position, 1, width), places(position, 1, width))
    return {
        "pick": rows_of(pick, Z * piece),
        "select": rows_of(select, columns * sent),
        "lines": rows_of(places(position, lines, 1), count),
        "turned": rows_of(turned, count),
        "flip": rows_of(flip, count),
        "flipped": flipped,
        "side": mine[:, 1],
        "kind": kind,
        "corner": rows_of(ends.reshape(-1) * (4 * lines) + np.arange(4 * lines, dtype=np.int32), 8 * lines),
        "quarter": mine[:, 3],
        "quarter_corner": my_corners[..., 3].T,
        "row": row,
    }


def rows_of(index, count):
    return (index[:, None] == jnp.arange(count)[None, :]).astype(bf16)


def take_rows(choice, rows):
    return jnp.dot(choice, rows, preferred_element_type=f32).astype(bf16)


def turn_channels(lines, quarter):
    half = lines.shape[-1] // 2
    first, second = lines[..., :half], lines[..., half:]
    quarter = quarter.reshape(quarter.shape + (1,) * (lines.ndim - quarter.ndim))
    odd = quarter % 2 == 1
    lead = jnp.where(odd, second, first)
    trail = jnp.where(odd, first, second)
    lead = jnp.where((quarter == 1) | (quarter == 2), -lead, lead)
    trail = jnp.where((quarter == 2) | (quarter == 3), -trail, trail)
    return jnp.concatenate([lead, trail], axis=-1)


def to_here(lines, plan, order="flip"):
    sides = plan["quarter"].shape[0]
    rows = take_rows(plan[order], lines.reshape(-1, lines.shape[-1]))
    return turn_channels(rows.reshape(sides, -1, lines.shape[-1]), plan["quarter"])


def to_neighbour(lines, plan, order="flip"):
    sides = plan["quarter"].shape[0]
    rows = take_rows(plan[order], lines.reshape(-1, lines.shape[-1]))
    return turn_channels(rows.reshape(sides, -1, lines.shape[-1]), (4 - plan["quarter"]) % 4)


def outer_lines(field, margin, row):
    tiles, rows, columns, channels = field.shape
    strip = rows - 2 * margin
    width = ROWS * strip
    unit = np.arange(UNITS)[:, None, None]
    cell = np.arange(strip)[None, :, None]
    tile = np.arange(tiles)[None, None, :] * (rows * columns)
    target = np.arange(ROWS)[:, None, None, None]
    last = width + 2 * margin - 1
    sides = np.stack([unit + tile, last - unit + tile], axis=-1) + (margin + cell)[..., None] * columns

    def index_of(line):
        ends = tile + line * columns + margin + target * strip + cell
        return np.concatenate([ends.reshape(-1), sides.reshape(-1)]).astype(np.int32)

    index = jnp.where(row == ROWS - 1, index_of(rows - 1 - unit), index_of(unit))
    chosen = take_rows(rows_of(index, tiles * rows * columns), field.reshape(-1, channels))
    cut = ROWS * UNITS * strip * tiles
    return chosen[:cut].reshape(ROWS, -1, channels), chosen[cut:]


def own_borders(field, plan):
    tiles, rows, columns, channels = field.shape
    strip = rows - 2
    width = ROWS * strip
    row = plan["row"]
    side = np.arange(4)[None, :, None]
    tile = np.arange(tiles)[:, None, None] * (rows * columns)

    def places(at):
        end = np.where(side == 0, 1 + at, (rows - 1) * columns + 1 + at)
        along = (1 + at) * columns + np.where(side == 2, 0, width + 1)
        index = tile + np.where(side < 2, end, along)
        owner = np.where(side < 2, side * (ROWS - 1), at // strip) + 0 * tile
        return index.reshape(-1).astype(np.int32), owner.reshape(-1).astype(np.int32)

    at = np.arange(width)[None, None, :]
    straight, owner = places(at)
    turned, owner_turned = places(width - 1 - at)
    index = jnp.where(plan["flipped"], turned, straight)
    off = np.where(side < 2, 0, strip * columns) + 0 * tile + 0 * at
    index = index - row * off.reshape(-1).astype(np.int32)
    index = jnp.where(jnp.where(plan["flipped"], owner_turned, owner) == row, index, -1)
    chosen = take_rows(rows_of(index, tiles * rows * columns), field.reshape(-1, channels))
    return turn_channels(chosen.reshape(tiles * 4, width, channels), (4 - plan["quarter"]) % 4)


def share_ends(ends):
    return lax.all_to_all(ends, ROW_AXES, 0, 0, tiled=True)


def offer(ends, sides, tiles):
    channels = sides.shape[-1]
    half = sides.shape[0] // 2
    piece = 4 * half
    held = jnp.concatenate([ends[0], ends[ROWS - 1], sides], axis=0)
    order = np.arange(half, dtype=np.int32)[:, None]
    order = np.concatenate(
        [order, half + order, 2 * half + 2 * order, 2 * half + 2 * order + 1], axis=1
    ).reshape(-1)
    everywhere = np.tile(order, Z)
    spread = take_rows(rows_of(everywhere, piece), held).reshape(Z, piece, channels)
    return spread, take_rows(rows_of(order[: piece // UNITS], piece), held)


def exchange(spread, first_own, tiles, plan, rider=None):
    lines = tiles * 4
    line, channels = first_own.shape
    piece = UNITS * line
    width = ROWS * line // lines
    gathered = lax.all_to_all(spread, "z", 0, 0, tiled=True).reshape(Z * piece, channels)
    sent = take_rows(plan["pick"], gathered).reshape(XH * CORE, -1, channels)
    arrived = lax.all_to_all(sent, COLUMN_AXES, 0, 0, tiled=True).reshape(-1, channels)
    mine = jnp.concatenate([take_rows(plan["select"], arrived), first_own], axis=0)
    count = mine.shape[0]
    mine = jnp.broadcast_to(mine[None], (ROWS,) + mine.shape)
    if rider is not None:
        mine = jnp.concatenate([mine, rider], axis=1)
    whole = lax.all_to_all(mine, ROW_AXES, 0, 0, tiled=True)
    first = whole[:, :line].reshape(ROWS * line, channels)
    second = whole[:, line : 2 * line].reshape(ROWS * line, channels)
    own = whole[:, piece + 4 * lines : count].reshape(ROWS * line, channels)
    corner = whole[:: ROWS - 1, piece : piece + 4 * lines].reshape(8 * lines, channels)
    corner = take_rows(plan["corner"], corner).reshape(2, 2, lines, channels)
    corner = turn_channels(corner, plan["quarter_corner"][:, None])
    return (
        to_here(first, plan, "turned"),
        take_rows(plan["lines"], first).reshape(lines, width, channels),
        take_rows(plan["lines"], second).reshape(lines, width, channels),
        to_neighbour(own, plan, "turned"),
        corner,
        whole[:, count:],
    )


def by_side(cells, plan):
    blocks = [
        jnp.where((plan["side"] == side)[:, None, None], cells, jnp.zeros((), cells.dtype))
        for side in range(4)
    ]
    return jnp.concatenate(blocks, axis=-1)


def edge_terms(patch_ref, kind_ref, weight_ref, out_ref, cells_ref):
    depths, lines = patch_ref.shape[:2]
    width = patch_ref.shape[2] - 2
    for depth in range(depths):
        for line in range(lines):
            cells = patch_ref[depth, line]
            for tap in range(3):
                cells_ref[depth * 3 + tap, line * width : (line + 1) * width] = shifted(cells, tap)
    part = lines * width // 2
    for half in range(2):
        total = None
        for depth in range(depths):
            for tap in range(3):
                cells = cells_ref[depth * 3 + tap, half * part : (half + 1) * part]
                places = ((depth, tap), (2 - depth, tap), (tap, depth), (tap, 2 - depth))
                for side, (a, b) in enumerate(places):
                    term = jnp.dot(
                        cells * kind_ref[side, half * part : (half + 1) * part],
                        weight_ref[a, b],
                        preferred_element_type=f32,
                    )
                    total = term if total is None else total + term
        out_ref[half * part : (half + 1) * part] = total


def neighbour_edge(edge, inner, own, corner, kernel_weight, plan):
    lines, width, channels = own.shape
    patch = jnp.stack(
        [
            jnp.pad(own, ((0, 0), (1, 1), (0, 0))),
            jnp.concatenate([corner[0, 0][:, None], edge, corner[1, 0][:, None]], axis=1),
            jnp.concatenate([corner[0, 1][:, None], inner, corner[1, 1][:, None]], axis=1),
        ]
    )
    total = pl.pallas_call(
        edge_terms,
        out_shape=jax.ShapeDtypeStruct((lines * width, channels), f32),
        in_specs=[WHOLE] * 3,
        out_specs=WHOLE,
        scratch_shapes=[pltpu.VMEM((9, lines * width, channels), bf16)],
        compiler_params=ROOM,
        cost_estimate=CHEAP,
    )(patch, plan["kind"], kernel_weight)
    return total.reshape(lines, width, channels), patch


def neighbour_border(grads, kernel_weight, plan):
    width = grads.shape[1]
    w = kernel_weight
    spread = by_side(jnp.pad(grads, ((0, 0), (1, 1), (0, 0))), plan)
    total = None
    for tap in range(3):
        weights = jnp.concatenate(
            [w[0, 2 - tap], w[2, 2 - tap], w[2 - tap, 0], w[2 - tap, 2]], axis=1
        )
        term = lax.dot_general(
            spread[:, tap : tap + width],
            weights,
            (((2,), (1,)), ((), ())),
            preferred_element_type=f32,
        )
        total = term if total is None else total + term
    return total


def own_part(lines, margin, plan):
    strip = lines.shape[1] // ROWS
    padded = jnp.pad(lines, ((0, 0), (margin, margin), (0, 0)))
    return lax.dynamic_slice_in_dim(padded, plan["row"] * strip, strip + 2 * margin, 1)


def with_ghosts(strips, ghosts, margin, plan):
    row = plan["row"]
    above = jnp.where(row == 0, ghosts[:, 0], strips[:, margin - 1])
    below = jnp.where(row == ROWS - 1, ghosts[:, 1], strips[:, -margin])
    middle = jnp.concatenate(
        [strips[:, : margin - 1], above[:, None], strips[:, margin:-margin], below[:, None]]
        + ([strips[:, -margin + 1 :]] if margin > 1 else []),
        axis=1,
    )
    left = own_part(ghosts[:, 2], margin, plan)
    right = own_part(ghosts[:, 3], margin, plan)
    return jnp.concatenate([left[:, :, None], middle, right[:, :, None]], axis=2)


def add_borders(interior, routed, margin, plan):
    row = plan["row"]
    routed = routed.astype(f32)
    rows = interior.shape[1]
    index = jnp.arange(rows)[None, :, None, None]
    top = jnp.where((row == 0) & (index == margin), routed[:, 0][:, None], 0.0)
    bottom = jnp.where(
        (row == ROWS - 1) & (index == rows - 1 - margin), routed[:, 1][:, None], 0.0
    )
    column = jnp.arange(interior.shape[2])[None, None, :, None]
    left = own_part(routed[:, 2], margin, plan)[:, :, None]
    right = own_part(routed[:, 3], margin, plan)[:, :, None]
    sides = jnp.where(column == 0, left, 0.0) + jnp.where(
        column == interior.shape[2] - 1, right, 0.0
    )
    return interior + top + bottom + sides


def inside(rows, margin, width, plan):
    strip = width // ROWS
    place = plan["row"] * strip - margin + jnp.arange(rows)
    return ((place >= 0) & (place < width))[None, :, None, None]


def shifted(field, tap):
    return field.astype(f32)[tap : tap + field.shape[0] - 2].astype(field.dtype)


def convolve_cells(back, padded_ref, weight_ref, out_ref, cells_ref):
    tiles, rows, columns = out_ref.shape[:3]
    step = tiles * columns
    for row in range(rows + 2):
        for tile in range(tiles):
            at = row * step + tile * columns
            line = padded_ref[tile, row]
            for tap in range(3):
                cells_ref[tap, at : at + columns] = shifted(line, tap)
    for row in range(0, rows, 2):
        total = None
        for a in range(3):
            for b in range(3):
                cells = cells_ref[b, (row + a) * step : (row + a + 2) * step]
                weight = weight_ref[2 - a, 2 - b] if back else weight_ref[a, b]
                term = lax.dot_general(
                    cells,
                    weight,
                    (((1,), (1 if back else 0,)), ((), ())),
                    preferred_element_type=f32,
                )
                total = term if total is None else total + term
        for half in range(2):
            for tile in range(tiles):
                at = half * step + tile * columns
                out_ref[tile, row + half] = total[at : at + columns]


WHOLE = pl.BlockSpec(memory_space=pltpu.VMEM)
ROOM = pltpu.CompilerParams(vmem_limit_bytes=40 * 2**20)
CHEAP = pl.CostEstimate(flops=1000, bytes_accessed=1000, transcendentals=0)


def convolve(padded, kernel_weight, back=False):
    tiles, rows, columns, channels = padded.shape
    return pl.pallas_call(
        functools.partial(convolve_cells, back),
        out_shape=jax.ShapeDtypeStruct((tiles, rows - 2, columns - 2, channels), f32),
        in_specs=[WHOLE] * 2,
        out_specs=WHOLE,
        scratch_shapes=[pltpu.VMEM((3, tiles * rows * (columns - 2), channels), bf16)],
        compiler_params=ROOM,
        cost_estimate=CHEAP,
    )(padded, kernel_weight)


def with_columns(grads, before, after):
    return jnp.pad(grads, ((0, 0), (0, 0), (before, after), (0, 0)))


def strip_terms(padded_ref, grads_ref, out_ref, cells_ref, rows_ref):
    tiles, rows, columns = grads_ref.shape[:3]
    for row in range(rows + 2):
        for tile in range(tiles):
            at = (row * tiles + tile) * columns
            line = padded_ref[tile, row]
            for tap in range(3):
                cells_ref[tap, at : at + columns] = shifted(line, tap)
            if row < rows:
                rows_ref[at : at + columns] = grads_ref[tile, row]
    grads = rows_ref[...]
    step = tiles * columns
    for a in range(3):
        for b in range(3):
            out_ref[a * 3 + b] = lax.dot_general(
                cells_ref[b, a * step : (a + rows) * step],
                grads,
                (((0,), (0,)), ((), ())),
                preferred_element_type=f32,
            )


def border_terms(patch_ref, grads_ref, edges_ref, out_ref):
    depths, lines = patch_ref.shape[:2]
    width, channels = patch_ref.shape[2] - 2, patch_ref.shape[3]
    for depth in range(depths):
        for line in range(lines):
            cells = patch_ref[depth, line]
            for tap in range(3):
                edges_ref[tap, line * width : (line + 1) * width] = shifted(cells, tap)
        for tap in range(3):
            term = lax.dot_general(
                edges_ref[tap],
                grads_ref[...],
                (((0,), (0,)), ((), ())),
                preferred_element_type=f32,
            )
            places = ((depth, tap), (2 - depth, tap), (tap, depth), (tap, 2 - depth))
            for side, (a, b) in enumerate(places):
                out_ref[a * 3 + b] += term[:, side * channels : (side + 1) * channels]


def weight_grad(padded, grads, patch=None, edge_grads=None):
    tiles, rows, columns, channels = grads.shape
    scratch = [
        pltpu.VMEM((3, tiles * (rows + 2) * columns, channels), bf16),
        pltpu.VMEM((tiles * rows * columns, channels), bf16),
    ]
    operands = [padded, grads]
    if patch is None:
        kernel = strip_terms
    else:
        operands += [patch, edge_grads]
        scratch.append(pltpu.VMEM((3, edge_grads.shape[0], channels), bf16))

        def kernel(padded_ref, grads_ref, patch_ref, edge_ref, out_ref, cells, rows, edges):
            strip_terms(padded_ref, grads_ref, out_ref, cells, rows)
            border_terms(patch_ref, edge_ref, edges, out_ref)

    return pl.pallas_call(
        kernel,
        out_shape=jax.ShapeDtypeStruct((9, channels, channels), f32),
        in_specs=[WHOLE] * len(operands),
        out_specs=WHOLE,
        scratch_shapes=scratch,
        compiler_params=ROOM,
        cost_estimate=CHEAP,
    )(*operands)


def grouped_cells(field):
    tiles, rows, columns, channels = field.shape
    return field.reshape(tiles, rows // 2, 2, columns // 2, 2, channels)


def strided_shrink(field, kernel_weight):
    grouped = grouped_cells(field)
    total = None
    for row_tap in range(2):
        for col_tap in range(2):
            term = jnp.dot(
                grouped[:, :, row_tap, :, col_tap],
                kernel_weight[row_tap, col_tap],
                preferred_element_type=f32,
            )
            total = term if total is None else total + term
    return total


def upsample_back(grads, kernel_weight):
    tiles, rows, columns, channels = grads.shape
    stacked = []
    for row_tap in range(2):
        pieces = [
            lax.dot_general(
                grads,
                kernel_weight[row_tap, col_tap],
                (((3,), (1,)), ((), ())),
                preferred_element_type=f32,
            )
            for col_tap in range(2)
        ]
        stacked.append(jnp.stack(pieces, axis=3))
    return jnp.stack(stacked, axis=2).reshape(tiles, rows * 2, columns * 2, kernel_weight.shape[2])


def down_terms(cells_ref, grads_ref, out_ref):
    for tap in range(cells_ref.shape[0]):
        out_ref[tap] = lax.dot_general(
            cells_ref[tap],
            grads_ref[...],
            (((0,), (0,)), ((), ())),
            preferred_element_type=f32,
        )


def down_grad(field, grads):
    channels = field.shape[-1]
    cells = grouped_cells(field).transpose(2, 4, 0, 1, 3, 5).reshape(4, -1, channels)
    return pl.pallas_call(
        down_terms,
        out_shape=jax.ShapeDtypeStruct((4, channels, channels), f32),
        in_specs=[WHOLE] * 2,
        out_specs=WHOLE,
        compiler_params=ROOM,
        cost_estimate=CHEAP,
    )(cells, grads.reshape(-1, channels))


def silu(value):
    return value * jax.nn.sigmoid(value)


def silu_slope(value):
    sigma = jax.nn.sigmoid(value)
    return sigma * (1.0 + value * (1.0 - sigma))


SWAP = [(0, 1), (1, 0)]


def sum_pair(blocks):
    channels = blocks[0].shape[-1]
    core = lax.axis_index("c")
    rows = jnp.concatenate([block.reshape(-1, channels) for block in blocks], axis=0)
    first, second = rows[: rows.shape[0] // 2], rows[rows.shape[0] // 2 :]
    sent = jnp.where(core == 0, second, first).astype(bf16)
    held = jnp.where(core == 0, first, second) + lax.ppermute(sent, "c", SWAP).astype(f32)
    return held.astype(bf16).reshape(ROWS, -1, channels)


def sum_shards(held, factor):
    channels = held.shape[-1]
    held = held.astype(f32).sum(0)
    held = held.astype(bf16).reshape(XH * Z, -1, channels)
    held = lax.all_to_all(held, ("xh", "z"), 0, 0, tiled=True).astype(f32).sum(0)
    held = (held * factor).astype(bf16)
    return broadcast_all(held, ("xh", "z"), XH * Z).reshape(-1, channels)


def gather_sums(held, beside):
    channels = held.shape[-1]
    core = lax.axis_index("c")
    held = broadcast_all(held, ROW_AXES, ROWS).reshape(-1, channels)
    held, beside = lax.optimization_barrier((held, beside))
    other = lax.ppermute(held, "c", SWAP)
    first = jnp.where(core == 0, held, other)
    second = jnp.where(core == 0, other, held)
    both = jnp.concatenate([first, second], axis=0).astype(f32)
    return both.reshape(-1, channels, channels), beside


def body(activations, matching, first_kernel_weight, conv_second, reduce_kernel_weight, cotangent):
    tiles, strip, width, channels = activations.shape
    factor = 1.0 / math.sqrt(matching.shape[0] * width * width)

    first_rows = jnp.concatenate(
        [activations[:, :4].reshape(tiles, 4 * width, channels), cotangent[:, 0]], axis=1
    )
    last_rows = jnp.concatenate(
        [activations[:, -4:].reshape(tiles, 4 * width, channels), cotangent[:, -1]], axis=1
    )
    def sides_of(lines):
        return lines.reshape(tiles, 4, width, channels)

    ends, sides = outer_lines(activations, 0, lax.axis_index(ROW_AXES))
    pieces, first_own = offer(share_ends(ends), sides, tiles)
    pieces, first_rows, last_rows, matching = lax.optimization_barrier(
        (pieces, first_rows, last_rows, matching)
    )
    plan = routing(matching, strip, channels)
    ghosts, edge, inner, own, corner, _ = exchange(pieces, first_own, tiles, plan)
    above = lax.ppermute(last_rows, ROW_AXES, [(i, i + 1) for i in range(ROWS - 1)])
    below = lax.ppermute(first_rows, ROW_AXES, [(i + 1, i) for i in range(ROWS - 1)])
    cells = 4 * width
    wide_input = jnp.concatenate(
        [
            above[:, :cells].reshape(tiles, 4, width, channels),
            activations,
            below[:, :cells].reshape(tiles, 4, width, channels),
        ],
        axis=1,
    )
    wide_cotangent = jnp.concatenate(
        [above[:, None, cells:], cotangent, below[:, None, cells:]], axis=1
    )

    edge_first, edge_cells = neighbour_edge(edge, inner, own, corner, first_kernel_weight, plan)
    padded_input = with_ghosts(wide_input, sides_of(ghosts), 4, plan)
    pre_first = convolve(padded_input, first_kernel_weight)
    hidden_first = jnp.where(
        inside(strip + 6, 3, width, plan), silu(pre_first).astype(bf16), jnp.zeros((), bf16)
    )

    ghosts = sides_of(to_here(silu(edge_first).astype(bf16), plan))
    padded_hidden = with_ghosts(hidden_first, ghosts, 3, plan)
    pre_second = convolve(padded_hidden, conv_second)
    hidden_second = silu(pre_second[:, 2:-2]).astype(bf16)
    output = strided_shrink(hidden_second, reduce_kernel_weight).astype(bf16)
    grad_second = (
        upsample_back(wide_cotangent, reduce_kernel_weight) * silu_slope(pre_second)
    ).astype(bf16)

    spread = convolve(with_columns(grad_second, 2, 2 + EXTRA), conv_second, True)
    narrow = spread.astype(bf16)
    ends, sides = outer_lines(narrow, 1, plan["row"])
    pieces, first_own = offer(share_ends(ends), sides, tiles)
    pieces, held_spread, held_narrow = lax.optimization_barrier((pieces, spread, narrow))

    edge_slope = silu_slope(edge_first)
    slope_first = silu_slope(pre_first[:, 2:-2])
    own_grad = (held_spread[:, 1:-1, 1 : width + 1] * slope_first[:, 1:-1]).astype(bf16)
    border_grad = (own_borders(held_narrow, plan).astype(f32) * edge_slope).astype(bf16)
    edge_grad = by_side(border_grad, plan).reshape(tiles * 4 * width, 4 * channels)
    parts = sum_pair(
        [
            weight_grad(padded_input[:, 3:-3], own_grad, edge_cells, edge_grad),
            weight_grad(padded_hidden[:, 2:-2], grad_second[:, 2:-2]),
            down_grad(hidden_second, cotangent),
        ]
    )

    routed, _, inner, own, corner, parts = exchange(
        pieces, first_own, tiles, plan, parts
    )
    routed = sides_of(routed)
    grad_first_hidden = add_borders(spread[:, :, 1 : width + 1], routed, 1, plan)
    grad_first = jnp.where(
        inside(strip + 2, 1, width, plan),
        (grad_first_hidden * slope_first).astype(bf16),
        jnp.zeros((), bf16),
    )

    place = jnp.arange(width)[None, :, None]
    corner = corner.astype(f32)
    edge_hidden = (
        inner.astype(f32)
        + own.astype(f32)
        + jnp.where(place == 0, corner[0, 0][:, None], 0.0)
        + jnp.where(place == width - 1, corner[1, 0][:, None], 0.0)
    )
    edge_grad = (edge_hidden * edge_slope).astype(bf16)
    routed = sides_of(to_here(neighbour_border(edge_grad, first_kernel_weight, plan).astype(bf16), plan))
    spread = convolve(with_columns(grad_first, 1, 1), first_kernel_weight, True)
    shards, spread = lax.optimization_barrier((sum_shards(parts, factor), spread))
    grad_activations = add_borders(spread, routed, 0, plan).astype(bf16)
    summed, (output, grad_activations) = gather_sums(shards, (output, grad_activations))
    square = (channels, channels)
    return (
        output,
        grad_activations,
        summed[:9].reshape((3, 3) + square),
        summed[9:18].reshape((3, 3) + square),
        summed[18:].reshape((2, 2) + square),
    )


def solution(mesh):
    fine = Mesh(mesh.devices.reshape(XH, Z, CORE, Y, XL), TILE_AXES + ROW_AXES)
    placed = P(TILE_AXES, ROW_AXES, None, None)
    return jax.shard_map(
        body,
        mesh=fine,
        in_specs=(placed, P(), P(), P(), P(), placed),
        out_specs=(placed, placed, P(), P(), P()),
        check_vma=False,
    )
```

profile of v0, /device:TPU:1, one launch (start us, length us, event | category | flops | bytes accessed | tf_op | source)
XLA Modules:
  0.0 304.0 jit_solution(14985073864536611745)
XLA Ops:
  1.4 1.5 fusion.38
  3.6 5.9 %all-to-all-start = ((bf16[8,36,256]{2,1,0:T(8,128)(2,1)}), bf16[8,36,256]{2,1,0:T(8,128)(2,1)S(1)}, u32[]{:S(2)}, u32[]{:S(2)}) async-start(bf16[8,36,256]{2,1,0:T(8,128)(2,1)} %reshape.748), calls=%async_computation | async-start | bytes 327680 | tf_op jit(solution)/shard_map/all_to_all | solution.py:190
  10.4 4.9 %all-to-all-done = bf16[8,36,256]{2,1,0:T(8,128)(2,1)S(1)} async-done(((bf16[8,36,256]{2,1,0:T(8,128)(2,1)}), bf16[8,36,256]{2,1,0:T(8,128)(2,1)S(1)}, u32[]{:S(2)}, u32[]{:S(2)}) %all-to-all-start) | async-done | bytes 147488 | tf_op jit(solution)/shard_map/all_to_all | solution.py:190
  15.3 1.2 convolution_convert_fusion.1
  19.0 1.3 collective-permute-start.1
  20.3 4.0 %collective-permute-start = (bf16[3,216,256]{2,1,0:T(8,128)(2,1)S(1)}, bf16[3,216,256]{2,1,0:T(8,128)(2,1)S(1)}, u32[]{:S(2)}, u32[]{:S(2)}) collective-permute-start(bf16[3,216,256]{2,1,0:T(8,128)(2,1)S(1)} %pad_maximum_fusion.10), channel_id=1, source_target_pairs={{0,1},{1,2},{2,3},{3,4},{4,5},{5,6},{6,7},{8,9},{9,10},{10,11},{11... | collective-permute-start | bytes 995336 | tf_op jit(solution)/shard_map/ppermute | solution.py:600
  25.2 8.2 %all-to-all-start.1 = ((bf16[8,144,256]{2,1,0:T(8,128)(2,1)}), bf16[8,144,256]{2,1,0:T(8,128)(2,1)S(1)}, u32[]{:S(2)}, u32[]{:S(2)}) async-start(bf16[8,144,256]{2,1,0:T(8,128)(2,1)} %bitcast.3), calls=%async_computation.1 | async-start | bytes 1179648 | tf_op jit(solution)/shard_map/all_to_all | solution.py:212
  38.5 11.2 %all-to-all-done.1 = bf16[8,144,256]{2,1,0:T(8,128)(2,1)S(1)} async-done(((bf16[8,144,256]{2,1,0:T(8,128)(2,1)}), bf16[8,144,256]{2,1,0:T(8,128)(2,1)S(1)}, u32[]{:S(2)}, u32[]{:S(2)}) %all-to-all-start.1) | async-done | bytes 589856 | tf_op jit(solution)/shard_map/all_to_all | solution.py:212
  49.6 1.5 fusion.17
  51.2 7.6 %all-to-all-start.2 = ((bf16[4,192,256]{2,1,0:T(8,128)(2,1)}), bf16[4,192,256]{2,1,0:T(8,128)(2,1)S(1)}, u32[]{:S(2)}, u32[]{:S(2)}) async-start(bf16[4,192,256]{2,1,0:T(8,128)(2,1)} %bitcast.43), calls=%async_computation.2 | async-start | bytes 786432 | tf_op jit(solution)/shard_map/all_to_all | solution.py:214
  58.8 8.0 %all-to-all-done.2 = bf16[4,192,256]{2,1,0:T(8,128)(2,1)S(1)} async-done(((bf16[4,192,256]{2,1,0:T(8,128)(2,1)}), bf16[4,192,256]{2,1,0:T(8,128)(2,1)S(1)}, u32[]{:S(2)}, u32[]{:S(2)}) %all-to-all-start.2) | async-done | bytes 393248 | tf_op jit(solution)/shard_map/all_to_all | solution.py:214
  68.2 4.4 %all-to-all-start.3 = ((bf16[8,264,256]{2,1,0:T(8,128)(2,1)}), bf16[8,264,256]{2,1,0:T(8,128)(2,1)}, u32[]{:S(2)}, u32[]{:S(2)}) async-start(bf16[8,264,256]{2,1,0:T(8,128)(2,1)} %broadcast_in_dim.566), calls=%async_computation.3 | async-start | bytes 2162688 | tf_op jit(solution)/shard_map/all_to_all | solution.py:220
  75.7 12.1 %all-to-all-done.3 = bf16[8,264,256]{2,1,0:T(8,128)(2,1)} async-done(((bf16[8,264,256]{2,1,0:T(8,128)(2,1)}), bf16[8,264,256]{2,1,0:T(8,128)(2,1)}, u32[]{:S(2)}, u32[]{:S(2)}) %all-to-all-start.3) | async-done | bytes 1081376 | tf_op jit(solution)/shard_map/all_to_all | solution.py:220
  87.8 1.2 fusion.171
  89.0 1.2 fusion.26
  90.1 1.2 fusion.23
  96.5 2.9 shard_map.317
  102.7 1.7 pad_maximum_fusion.5.padded_ref
  104.4 2.1 reshape.757
  106.6 1.3 copy-done.11
  107.8 2.2 shard_map.318
  112.6 1.9 shard_map.319
  115.6 1.4 pad.41.padded_ref
  117.7 1.3 copy-done.19
  119.0 1.2 copy-done.20
  120.2 2.0 shard_map.320
  124.6 1.4 add_multiply_fusion
  129.4 4.0 %all-to-all-start.4 = ((bf16[8,36,256]{2,1,0:T(8,128)(2,1)}), bf16[8,36,256]{2,1,0:T(8,128)(2,1)}, u32[]{:S(2)}, u32[]{:S(2)}) async-start(bf16[8,36,256]{2,1,0:T(8,128)(2,1)} %reshape.777), calls=%async_computation.4 | async-start | bytes 327680 | tf_op jit(solution)/shard_map/all_to_all | solution.py:190
  135.5 1.5 shard_map.322
  138.0 1.9 reshape.786
  140.0 1.8 copy.136
  143.1 2.0 convolution_convert_fusion
  145.1 4.6 %all-to-all-start.5 = ((bf16[8,144,256]{2,1,0:T(8,128)(2,1)}), bf16[8,144,256]{2,1,0:T(8,128)(2,1)}, u32[]{:S(2)}, u32[]{:S(2)}) async-start(bf16[8,144,256]{2,1,0:T(8,128)(2,1)} %bitcast.346), calls=%async_computation.5 | async-start | bytes 1179648 | tf_op jit(solution)/shard_map/all_to_all | solution.py:212
  149.8 2.0 fusion.29
  155.1 5.1 %shard_map.321 = f32[9,256,256]{2,1,0:T(8,128)S(1)} custom-call(bf16[3,8,50,256]{3,2,1,0:T(8,128)(2,1)S(1)} %copy-done.24, bf16[3,6,48,256]{3,2,1,0:T(8,128)(2,1)S(1)} %fusion.42.grads_ref, bf16[3,12,50,256]{3,2,1,0:T(8,128)(2,1)S(1)} %copy-done.10, bf16[576,1024]{1,0:T(8,128)(2,1)S(1)} %pad_maximum_fusion.6.edge_ref), custom_call_target="tpu_custom_call" | custom-call | flops 1000 | bytes 1000 | tf_op jit(solution)/shard_map/pallas_call | solution.py:467
  160.2 1.6 select_convert_fusion
  162.1 1.8 collective-permute-start.2
  163.8 3.3 %all-to-all-done.5 = bf16[8,144,256]{2,1,0:T(8,128)(2,1)} async-done(((bf16[8,144,256]{2,1,0:T(8,128)(2,1)}), bf16[8,144,256]{2,1,0:T(8,128)(2,1)}, u32[]{:S(2)}, u32[]{:S(2)}) %all-to-all-start.5) | async-done | bytes 589856 | tf_op jit(solution)/shard_map/all_to_all | solution.py:212
  167.1 2.6 fusion.18
  169.7 6.5 %all-to-all-start.6 = ((bf16[4,192,256]{2,1,0:T(8,128)(2,1)}), bf16[4,192,256]{2,1,0:T(8,128)(2,1)}, u32[]{:S(2)}, u32[]{:S(2)}) async-start(bf16[4,192,256]{2,1,0:T(8,128)(2,1)} %bitcast.348), calls=%async_computation.6 | async-start | bytes 786432 | tf_op jit(solution)/shard_map/all_to_all | solution.py:214
  176.2 1.6 convolution_convert_fusion.4
  177.8 6.6 %all-to-all-done.6 = bf16[4,192,256]{2,1,0:T(8,128)(2,1)} async-done(((bf16[4,192,256]{2,1,0:T(8,128)(2,1)}), bf16[4,192,256]{2,1,0:T(8,128)(2,1)}, u32[]{:S(2)}, u32[]{:S(2)}) %all-to-all-start.6) | async-done | bytes 393248 | tf_op jit(solution)/shard_map/all_to_all | solution.py:214
  184.4 1.3 convolution_convert_fusion.2
  186.5 2.9 add_convert_fusion
  189.5 1.7 pad_maximum_fusion.2
  191.2 5.3 %all-to-all-start.7 = ((bf16[8,616,256]{2,1,0:T(8,128)(2,1)}), bf16[8,616,256]{2,1,0:T(8,128)(2,1)}, u32[]{:S(2)}, u32[]{:S(2)}) async-start(bf16[8,616,256]{2,1,0:T(8,128)(2,1)} %pad_maximum_fusion.2), calls=%async_computation.7 | async-start | bytes 5046272 | tf_op jit(solution)/shard_map/all_to_all | solution.py:220
  199.8 27.1 %all-to-all-done.7 = bf16[8,616,256]{2,1,0:T(8,128)(2,1)} async-done(((bf16[8,616,256]{2,1,0:T(8,128)(2,1)}), bf16[8,616,256]{2,1,0:T(8,128)(2,1)}, u32[]{:S(2)}, u32[]{:S(2)}) %all-to-all-start.7) | async-done | bytes 2523168 | tf_op jit(solution)/shard_map/all_to_all | solution.py:220
  228.0 1.2 fusion.170
  235.6 1.6 slice_reduce_fusion
  237.9 4.3 %all-to-all-start.8 = ((bf16[16,22,256]{2,1,0:T(8,128)(2,1)}), bf16[16,22,256]{2,1,0:T(8,128)(2,1)}, u32[]{:S(2)}, u32[]{:S(2)}) async-start(bf16[16,22,256]{2,1,0:T(8,128)(2,1)} %reshape.791), calls=%async_computation.8 | async-start | bytes 393216 | tf_op jit(solution)/shard_map/all_to_all | solution.py:563
  242.3 1.8 slice_bitcast_fusion.5
  245.3 6.0 %all-to-all-done.8 = bf16[16,22,256]{2,1,0:T(8,128)(2,1)} async-done(((bf16[16,22,256]{2,1,0:T(8,128)(2,1)}), bf16[16,22,256]{2,1,0:T(8,128)(2,1)}, u32[]{:S(2)}, u32[]{:S(2)}) %all-to-all-start.8) | async-done | bytes 180256 | tf_op jit(solution)/shard_map/all_to_all | solution.py:563
  253.0 4.2 %all-to-all-start.9 = ((bf16[16,22,256]{2,1,0:T(8,128)(2,1)}), bf16[16,22,256]{2,1,0:T(8,128)(2,1)}, u32[]{:S(2)}, u32[]{:S(2)}) async-start(bf16[16,22,256]{2,1,0:T(8,128)(2,1)} %broadcast_in_dim.597), calls=%async_computation.9 | async-start | bytes 393216 | tf_op jit(solution)/shard_map/all_to_all | solution.py:24
  257.2 2.4 fusion.61
  261.0 1.2 shard_map.324
  262.3 3.9 %all-to-all-done.9 = bf16[16,22,256]{2,1,0:T(8,128)(2,1)} async-done(((bf16[16,22,256]{2,1,0:T(8,128)(2,1)}), bf16[16,22,256]{2,1,0:T(8,128)(2,1)}, u32[]{:S(2)}, u32[]{:S(2)}) %all-to-all-start.9) | async-done | bytes 180256 | tf_op jit(solution)/shard_map/all_to_all | solution.py:24
  267.1 1.2 broadcast_in_dim.611
  268.3 5.7 %all-to-all-start.10 = ((bf16[8,352,256]{2,1,0:T(8,128)(2,1)}), bf16[8,352,256]{2,1,0:T(8,128)(2,1)}, u32[]{:S(2)}, u32[]{:S(2)}) async-start(bf16[8,352,256]{2,1,0:T(8,128)(2,1)} %broadcast_in_dim.611), calls=%async_computation.10 | async-start | bytes 2883584 | tf_op jit(solution)/shard_map/all_to_all | solution.py:24
  274.0 1.7 fusion.40
  277.5 13.6 %all-to-all-done.10 = bf16[8,352,256]{2,1,0:T(8,128)(2,1)} async-done(((bf16[8,352,256]{2,1,0:T(8,128)(2,1)}), bf16[8,352,256]{2,1,0:T(8,128)(2,1)}, u32[]{:S(2)}, u32[]{:S(2)}) %all-to-all-start.10) | async-done | bytes 1441824 | tf_op jit(solution)/shard_map/all_to_all | solution.py:24
  291.0 4.0 %collective-permute-start.3 = (bf16[2816,256]{1,0:T(8,128)(2,1)}, bf16[2816,256]{1,0:T(8,128)(2,1)S(1)}, u32[]{:S(2)}, u32[]{:S(2)}) collective-permute-start(bf16[2816,256]{1,0:T(8,128)(2,1)} %bitcast.106), channel_id=1, source_target_pairs={{0,8},{8,0},{1,9},{9,1},{2,10},{10,2},{3,11},{11,3},{4,12},{12,4},... | collective-permute-start | bytes 4325384 | tf_op jit(solution)/shard_map/ppermute | solution.py:573
  295.0 3.1 %collective-permute-done.3 = bf16[2816,256]{1,0:T(8,128)(2,1)S(1)} collective-permute-done((bf16[2816,256]{1,0:T(8,128)(2,1)}, bf16[2816,256]{1,0:T(8,128)(2,1)S(1)}, u32[]{:S(2)}, u32[]{:S(2)}) %collective-permute-start.3) | collective-permute-done | bytes 1441824 | tf_op jit(solution)/shard_map/ppermute | solution.py:573
  298.1 1.7 broadcast_select_fusion.1
  301.3 2.5 fusion.169
  (418 shorter events, 61.1 us)
Async XLA Ops:
  0.6 8.9 %copy-start.32 = (bf16[3,6,48,256]{3,2,1,0:T(8,128)(2,1)S(1)}, bf16[3,6,48,256]{3,2,1,0:T(8,128)(2,1)}, u32[]{:S(2)}) copy-start(bf16[3,6,48,256]{3,2,1,0:T(8,128)(2,1)} %param.30) | copy-start | bytes 1327108
  1.4 8.2 %copy-start.26 = (bf16[3,3,24,256]{3,2,1,0:T(8,128)(2,1)S(1)}, bf16[3,3,24,256]{3,2,1,0:T(8,128)(2,1)}, u32[]{:S(2)}) copy-start(bf16[3,3,24,256]{3,2,1,0:T(8,128)(2,1)} %param.35) | copy-start | bytes 331780
  2.9 6.9 %copy-start.97 = (s32[360]{0:T(512)S(1)}, s32[360]{0:T(512)}, u32[]{:S(2)}) copy-start(s32[360]{0:T(512)} %constant.355.clone) | copy-start | bytes 4324
  2.9 6.9 %copy-start.98 = (s32[360]{0:T(512)S(1)}, s32[360]{0:T(512)}, u32[]{:S(2)}) copy-start(s32[360]{0:T(512)} %constant.356.clone) | copy-start | bytes 4324
  2.9 7.4 %copy-start.102 = (s32[4]{0:T(128)S(1)}, s32[4]{0:T(128)}, u32[]{:S(2)}) copy-start(s32[4]{0:T(128)} %constant.348.clone) | copy-start | bytes 52
  2.9 7.4 %copy-start.103 = (s32[4]{0:T(128)S(1)}, s32[4]{0:T(128)}, u32[]{:S(2)}) copy-start(s32[4]{0:T(128)} %constant.349.clone) | copy-start | bytes 52
  3.6 11.7 %all-to-all-start = ((bf16[8,36,256]{2,1,0:T(8,128)(2,1)}), bf16[8,36,256]{2,1,0:T(8,128)(2,1)S(1)}, u32[]{:S(2)}, u32[]{:S(2)}) async-start(bf16[8,36,256]{2,1,0:T(8,128)(2,1)} %reshape.748), calls=%async_computation | async-start | bytes 327680 | tf_op jit(solution)/shard_map/all_to_all | solution.py:190
  9.6 5.7 %copy-start.104 = (s32[1152]{0:T(1024)S(1)}, s32[1152]{0:T(1024)}, u32[]{:S(2)}) copy-start(s32[1152]{0:T(1024)} %constant.384) | copy-start | bytes 13828
  9.7 6.8 %copy-start.48 = (s32[96,4,4]{0,2,1:T(4,128)S(1)}, s32[96,4,4]{0,2,1:T(4,128)}, u32[]{:S(2)}) copy-start(s32[96,4,4]{0,2,1:T(4,128)} %param.31) | copy-start | bytes 18436
  16.6 18.6 %copy-start.107 = (s32[72]{0:T(128)S(1)}, s32[72]{0:T(128)}, u32[]{:S(2)}) copy-start(s32[72]{0:T(128)} %constant.386) | copy-start | bytes 868
  16.9 18.5 %copy-start.74 = (s32[576]{0:T(1024)S(1)}, s32[576]{0:T(1024)}, u32[]{:S(2)}) copy-start(s32[576]{0:T(1024)} %constant.352.clone) | copy-start | bytes 6916
  16.9 18.5 %copy-start.82 = (s32[576]{0:T(1024)S(1)}, s32[576]{0:T(1024)}, u32[]{:S(2)}) copy-start(s32[576]{0:T(1024)} %constant.351.clone) | copy-start | bytes 6916
  17.0 18.5 %copy-start.83 = (s32[576]{0:T(1024)S(1)}, s32[576]{0:T(1024)}, u32[]{:S(2)}) copy-start(s32[576]{0:T(1024)} %constant.353.clone) | copy-start | bytes 6916
  17.0 18.5 %copy-start.84 = (s32[576]{0:T(1024)S(1)}, s32[576]{0:T(1024)}, u32[]{:S(2)}) copy-start(s32[576]{0:T(1024)} %constant.357.clone) | copy-start | bytes 6916
  17.0 18.5 %copy-start.85 = (s32[576]{0:T(1024)S(1)}, s32[576]{0:T(1024)}, u32[]{:S(2)}) copy-start(s32[576]{0:T(1024)} %constant.358.clone) | copy-start | bytes 6916
  17.0 18.4 %copy-start.86 = (s32[576]{0:T(1024)S(1)}, s32[576]{0:T(1024)}, u32[]{:S(2)}) copy-start(s32[576]{0:T(1024)} %constant.359.clone) | copy-start | bytes 6916
  17.0 18.4 %copy-start.87 = (s32[576]{0:T(1024)S(1)}, s32[576]{0:T(1024)}, u32[]{:S(2)}) copy-start(s32[576]{0:T(1024)} %constant.360.clone) | copy-start | bytes 6916
  17.0 18.4 %copy-start.88 = (s32[576]{0:T(1024)S(1)}, s32[576]{0:T(1024)}, u32[]{:S(2)}) copy-start(s32[576]{0:T(1024)} %constant.361.clone) | copy-start | bytes 6916
  19.0 32.2 %copy-start.59 = (pred[12]{0:T(512)(128)(4,1)}, pred[12]{0:T(512)(128)(4,1)S(1)}, u32[]{:S(2)}) copy-start(pred[12]{0:T(512)(128)(4,1)S(1)} %get-tuple-element.112) | copy-start | bytes 40
  19.0 32.2 %copy-start.61 = (pred[12]{0:T(512)(128)(4,1)}, pred[12]{0:T(512)(128)(4,1)S(1)}, u32[]{:S(2)}) copy-start(pred[12]{0:T(512)(128)(4,1)S(1)} %get-tuple-element.113) | copy-start | bytes 40
  19.0 32.2 %copy-start.63 = (pred[12]{0:T(512)(128)(4,1)}, pred[12]{0:T(512)(128)(4,1)S(1)}, u32[]{:S(2)}) copy-start(pred[12]{0:T(512)(128)(4,1)S(1)} %get-tuple-element.114) | copy-start | bytes 40
  19.0 81.3 %copy-start.53 = (pred[12]{0:T(512)(128)(4,1)}, pred[12]{0:T(512)(128)(4,1)S(1)}, u32[]{:S(2)}) copy-start(pred[12]{0:T(512)(128)(4,1)S(1)} %get-tuple-element.118) | copy-start | bytes 40
  19.0 39.7 %collective-permute-start.1 = (bf16[3,216,256]{2,1,0:T(8,128)(2,1)S(1)}, bf16[3,216,256]{2,1,0:T(8,128)(2,1)S(1)}, u32[]{:S(2)}, u32[]{:S(2)}) collective-permute-start(bf16[3,216,256]{2,1,0:T(8,128)(2,1)S(1)} %pad_maximum_fusion.9), channel_id=1, source_target_pairs={{1,0},{2,1},{3,2},{4,3},{5,4},{6,5},{7,6},{9,8},{10,9},{11,10},{12... | collective-permute-start | bytes 995336 | tf_op jit(solution)/shard_map/ppermute | solution.py:601
  20.3 38.4 %collective-permute-start = (bf16[3,216,256]{2,1,0:T(8,128)(2,1)S(1)}, bf16[3,216,256]{2,1,0:T(8,128)(2,1)S(1)}, u32[]{:S(2)}, u32[]{:S(2)}) collective-permute-start(bf16[3,216,256]{2,1,0:T(8,128)(2,1)S(1)} %pad_maximum_fusion.10), channel_id=1, source_target_pairs={{0,1},{1,2},{2,3},{3,4},{4,5},{5,6},{6,7},{8,9},{9,10},{10,11},{11... | collective-permute-start | bytes 995336 | tf_op jit(solution)/shard_map/ppermute | solution.py:600
  25.2 24.5 %all-to-all-start.1 = ((bf16[8,144,256]{2,1,0:T(8,128)(2,1)}), bf16[8,144,256]{2,1,0:T(8,128)(2,1)S(1)}, u32[]{:S(2)}, u32[]{:S(2)}) async-start(bf16[8,144,256]{2,1,0:T(8,128)(2,1)} %bitcast.3), calls=%async_computation.1 | async-start | bytes 1179648 | tf_op jit(solution)/shard_map/all_to_all | solution.py:212
  33.7 33.1 %copy-start.99 = (s32[192]{0:T(256)}, s32[192]{0:T(256)S(1)}, u32[]{:S(2)}) copy-start(s32[192]{0:T(256)S(1)} %iota_add_fusion) | copy-start | bytes 2308
  34.1 59.9 %copy-start.67 = (pred[2,12]{1,0:T(4,128)(4,1)}, pred[2,12]{1,0:T(4,128)(4,1)S(1)}, u32[]{:S(2)}) copy-start(pred[2,12]{1,0:T(4,128)(4,1)S(1)} %get-tuple-element.131) | copy-start | bytes 76
  34.1 59.9 %copy-start.69 = (pred[2,12]{1,0:T(4,128)(4,1)}, pred[2,12]{1,0:T(4,128)(4,1)S(1)}, u32[]{:S(2)}) copy-start(pred[2,12]{1,0:T(4,128)(4,1)S(1)} %get-tuple-element.132) | copy-start | bytes 76
  34.1 59.9 %copy-start.71 = (pred[2,12]{1,0:T(4,128)(4,1)}, pred[2,12]{1,0:T(4,128)(4,1)S(1)}, u32[]{:S(2)}) copy-start(pred[2,12]{1,0:T(4,128)(4,1)S(1)} %get-tuple-element.133) | copy-start | bytes 76
  34.9 58.9 %copy-start.105 = (s32[48]{0:T(128)}, s32[48]{0:T(128)S(1)}, u32[]{:S(2)}) copy-start(s32[48]{0:T(128)S(1)} %iota_add_fusion.1) | copy-start | bytes 580
  36.1 55.2 %copy-start.76 = (s32[576]{0:T(1024)}, s32[576]{0:T(1024)S(1)}, u32[]{:S(2)}) copy-start(s32[576]{0:T(1024)S(1)} %get-tuple-element.129) | copy-start | bytes 6916
  36.1 63.4 %copy-start.78 = (s32[576]{0:T(1024)}, s32[576]{0:T(1024)S(1)}, u32[]{:S(2)}) copy-start(s32[576]{0:T(1024)S(1)} %get-tuple-element.130) | copy-start | bytes 6916
  36.2 15.0 %copy-start.80 = (s32[768]{0:T(1024)}, s32[768]{0:T(1024)S(1)}, u32[]{:S(2)}) copy-start(s32[768]{0:T(1024)S(1)} %eq.517) | copy-start | bytes 9220
  51.2 15.7 %all-to-all-start.2 = ((bf16[4,192,256]{2,1,0:T(8,128)(2,1)}), bf16[4,192,256]{2,1,0:T(8,128)(2,1)S(1)}, u32[]{:S(2)}, u32[]{:S(2)}) async-start(bf16[4,192,256]{2,1,0:T(8,128)(2,1)} %bitcast.43), calls=%async_computation.2 | async-start | bytes 786432 | tf_op jit(solution)/shard_map/all_to_all | solution.py:214
  58.8 9.5 %copy-start.43 = (bf16[3,216,256]{2,1,0:T(8,128)(2,1)}, bf16[3,216,256]{2,1,0:T(8,128)(2,1)S(1)}, u32[]{:S(2)}) copy-start(bf16[3,216,256]{2,1,0:T(8,128)(2,1)S(1)} %collective-permute-done.1) | copy-start | bytes 995332
  67.2 5.5 %copy-start.41 = (bf16[2,2,256,256]{3,2,1,0:T(8,128)(2,1)S(1)}, bf16[2,2,256,256]{3,2,1,0:T(8,128)(2,1)}, u32[]{:S(2)}) copy-start(bf16[2,2,256,256]{3,2,1,0:T(8,128)(2,1)} %param.34) | copy-start | bytes 1572868
  68.2 19.5 %all-to-all-start.3 = ((bf16[8,264,256]{2,1,0:T(8,128)(2,1)}), bf16[8,264,256]{2,1,0:T(8,128)(2,1)}, u32[]{:S(2)}, u32[]{:S(2)}) async-start(bf16[8,264,256]{2,1,0:T(8,128)(2,1)} %broadcast_in_dim.566), calls=%async_computation.3 | async-start | bytes 2162688 | tf_op jit(solution)/shard_map/all_to_all | solution.py:220
  74.9 15.2 %copy-start.34 = (bf16[3,192,256]{2,1,0:T(8,128)(2,1)}, bf16[3,192,256]{2,1,0:T(8,128)(2,1)S(1)}, u32[]{:S(2)}) copy-start(bf16[3,192,256]{2,1,0:T(8,128)(2,1)S(1)} %slice.512) | copy-start | bytes 884740
  95.0 4.4 %copy-start.9 = (bf16[3,12,50,256]{3,2,1,0:T(8,128)(2,1)}, bf16[3,12,50,256]{3,2,1,0:T(8,128)(2,1)S(1)}, u32[]{:S(2)}) copy-start(bf16[3,12,50,256]{3,2,1,0:T(8,128)(2,1)S(1)} %pad_maximum_fusion.7.patch_ref) | copy-start | bytes 2764804
  110.1 14.6 %copy-start.1 = (f32[3,12,48,256]{3,2,1,0:T(8,128)}, f32[3,12,48,256]{3,2,1,0:T(8,128)S(1)}, u32[]{:S(2)}) copy-start(f32[3,12,48,256]{3,2,1,0:T(8,128)S(1)} %shard_map.318) | copy-start | bytes 5308420
  129.4 12.4 %all-to-all-start.4 = ((bf16[8,36,256]{2,1,0:T(8,128)(2,1)}), bf16[8,36,256]{2,1,0:T(8,128)(2,1)}, u32[]{:S(2)}, u32[]{:S(2)}) async-start(bf16[8,36,256]{2,1,0:T(8,128)(2,1)} %reshape.777), calls=%async_computation.4 | async-start | bytes 327680 | tf_op jit(solution)/shard_map/all_to_all | solution.py:190
  140.0 9.8 %copy-start.89 = (s32[576]{0:T(1024)S(1)}, s32[576]{0:T(1024)}, u32[]{:S(2)}) copy-start(s32[576]{0:T(1024)} %get-tuple-element.128) | copy-start | bytes 6916
  145.1 22.0 %all-to-all-start.5 = ((bf16[8,144,256]{2,1,0:T(8,128)(2,1)}), bf16[8,144,256]{2,1,0:T(8,128)(2,1)}, u32[]{:S(2)}, u32[]{:S(2)}) async-start(bf16[8,144,256]{2,1,0:T(8,128)(2,1)} %bitcast.346), calls=%async_computation.5 | async-start | bytes 1179648 | tf_op jit(solution)/shard_map/all_to_all | solution.py:212
  155.1 5.1 %copy-start.8 = (f32[4,256,256]{2,1,0:T(8,128)}, f32[4,256,256]{2,1,0:T(8,128)S(1)}, u32[]{:S(2)}) copy-start(f32[4,256,256]{2,1,0:T(8,128)S(1)} %shard_map.323) | copy-start | bytes 3145732
  160.2 6.9 %copy-start.81 = (s32[768]{0:T(1024)S(1)}, s32[768]{0:T(1024)}, u32[]{:S(2)}) copy-start(s32[768]{0:T(1024)} %copy-done.80) | copy-start | bytes 9220
  162.1 24.4 %collective-permute-start.2 = (bf16[2816,256]{1,0:T(8,128)(2,1)}, bf16[2816,256]{1,0:T(8,128)(2,1)}, u32[]{:S(2)}, u32[]{:S(2)}) collective-permute-start(bf16[2816,256]{1,0:T(8,128)(2,1)} %select_convert_fusion), channel_id=1, source_target_pairs={{0,8},{8,0},{1,9},{9,1},{2,10},{10,2},{3,11},{11,3},{4,12},{12,4},... | collective-permute-start | bytes 4325384 | tf_op jit(solution)/shard_map/ppermute | solution.py:555
  169.7 14.7 %all-to-all-start.6 = ((bf16[4,192,256]{2,1,0:T(8,128)(2,1)}), bf16[4,192,256]{2,1,0:T(8,128)(2,1)}, u32[]{:S(2)}, u32[]{:S(2)}) async-start(bf16[4,192,256]{2,1,0:T(8,128)(2,1)} %bitcast.348), calls=%async_computation.6 | async-start | bytes 786432 | tf_op jit(solution)/shard_map/all_to_all | solution.py:214
  191.2 35.7 %all-to-all-start.7 = ((bf16[8,616,256]{2,1,0:T(8,128)(2,1)}), bf16[8,616,256]{2,1,0:T(8,128)(2,1)}, u32[]{:S(2)}, u32[]{:S(2)}) async-start(bf16[8,616,256]{2,1,0:T(8,128)(2,1)} %pad_maximum_fusion.2), calls=%async_computation.7 | async-start | bytes 5046272 | tf_op jit(solution)/shard_map/all_to_all | solution.py:220
  198.1 32.3 %copy-start.51 = (pred[48]{0:T(512)(128)(4,1)}, pred[48]{0:T(512)(128)(4,1)S(1)}, u32[]{:S(2)}) copy-start(pred[48]{0:T(512)(128)(4,1)S(1)} %get-tuple-element.144) | copy-start | bytes 148
  198.6 29.1 %copy-start.106 = (s32[48]{0:T(128)S(1)}, s32[48]{0:T(128)}, u32[]{:S(2)}) copy-start(s32[48]{0:T(128)} %copy-done.105) | copy-start | bytes 580
  198.6 29.3 %copy-start.68 = (pred[2,12]{1,0:T(4,128)(4,1)S(1)}, pred[2,12]{1,0:T(4,128)(4,1)}, u32[]{:S(2)}) copy-start(pred[2,12]{1,0:T(4,128)(4,1)} %copy-done.67) | copy-start | bytes 76
  198.6 29.3 %copy-start.70 = (pred[2,12]{1,0:T(4,128)(4,1)S(1)}, pred[2,12]{1,0:T(4,128)(4,1)}, u32[]{:S(2)}) copy-start(pred[2,12]{1,0:T(4,128)(4,1)} %copy-done.69) | copy-start | bytes 76
  198.6 29.3 %copy-start.72 = (pred[2,12]{1,0:T(4,128)(4,1)S(1)}, pred[2,12]{1,0:T(4,128)(4,1)}, u32[]{:S(2)}) copy-start(pred[2,12]{1,0:T(4,128)(4,1)} %copy-done.71) | copy-start | bytes 76
  198.9 30.3 %copy-start.77 = (s32[576]{0:T(1024)S(1)}, s32[576]{0:T(1024)}, u32[]{:S(2)}) copy-start(s32[576]{0:T(1024)} %copy-done.76) | copy-start | bytes 6916
  237.9 19.3 %copy-start.2 = (f32[3,12,48,256]{3,2,1,0:T(8,128)S(1)}, f32[3,12,48,256]{3,2,1,0:T(8,128)}, u32[]{:S(2)}) copy-start(f32[3,12,48,256]{3,2,1,0:T(8,128)} %copy-done.1) | copy-start | bytes 5308420
  237.9 19.3 %copy-start.52 = (pred[48]{0:T(512)(128)(4,1)S(1)}, pred[48]{0:T(512)(128)(4,1)}, u32[]{:S(2)}) copy-start(pred[48]{0:T(512)(128)(4,1)} %copy-done.51) | copy-start | bytes 148
  237.9 19.3 %copy-start.94 = (pred[8]{0:T(512)(128)(4,1)S(1)}, pred[8]{0:T(512)(128)(4,1)}, u32[]{:S(2)}) copy-start(pred[8]{0:T(512)(128)(4,1)} %get-tuple-element.145) | copy-start | bytes 28
  237.9 19.3 %copy-start.95 = (pred[8]{0:T(512)(128)(4,1)S(1)}, pred[8]{0:T(512)(128)(4,1)}, u32[]{:S(2)}) copy-start(pred[8]{0:T(512)(128)(4,1)} %get-tuple-element.146) | copy-start | bytes 28
  237.9 13.4 %all-to-all-start.8 = ((bf16[16,22,256]{2,1,0:T(8,128)(2,1)}), bf16[16,22,256]{2,1,0:T(8,128)(2,1)}, u32[]{:S(2)}, u32[]{:S(2)}) async-start(bf16[16,22,256]{2,1,0:T(8,128)(2,1)} %reshape.791), calls=%async_computation.8 | async-start | bytes 393216 | tf_op jit(solution)/shard_map/all_to_all | solution.py:563
  253.0 13.2 %all-to-all-start.9 = ((bf16[16,22,256]{2,1,0:T(8,128)(2,1)}), bf16[16,22,256]{2,1,0:T(8,128)(2,1)}, u32[]{:S(2)}, u32[]{:S(2)}) async-start(bf16[16,22,256]{2,1,0:T(8,128)(2,1)} %broadcast_in_dim.597), calls=%async_computation.9 | async-start | bytes 393216 | tf_op jit(solution)/shard_map/all_to_all | solution.py:24
  268.3 7.4 %copy-start.37 = (bf16[12,48,128]{2,1,0:T(8,128)(2,1)S(1)}, bf16[12,48,128]{2,1,0:T(8,128)(2,1)}, u32[]{:S(2)}) copy-start(bf16[12,48,128]{2,1,0:T(8,128)(2,1)} %get-tuple-element.126) | copy-start | bytes 442372
  268.3 7.4 %copy-start.38 = (bf16[12,48,128]{2,1,0:T(8,128)(2,1)S(1)}, bf16[12,48,128]{2,1,0:T(8,128)(2,1)}, u32[]{:S(2)}) copy-start(bf16[12,48,128]{2,1,0:T(8,128)(2,1)} %get-tuple-element.127) | copy-start | bytes 442372
  268.3 22.7 %all-to-all-start.10 = ((bf16[8,352,256]{2,1,0:T(8,128)(2,1)}), bf16[8,352,256]{2,1,0:T(8,128)(2,1)}, u32[]{:S(2)}, u32[]{:S(2)}) async-start(bf16[8,352,256]{2,1,0:T(8,128)(2,1)} %broadcast_in_dim.611), calls=%async_computation.10 | async-start | bytes 2883584 | tf_op jit(solution)/shard_map/all_to_all | solution.py:24
  291.0 7.1 %collective-permute-start.3 = (bf16[2816,256]{1,0:T(8,128)(2,1)}, bf16[2816,256]{1,0:T(8,128)(2,1)S(1)}, u32[]{:S(2)}, u32[]{:S(2)}) collective-permute-start(bf16[2816,256]{1,0:T(8,128)(2,1)} %bitcast.106), channel_id=1, source_target_pairs={{0,8},{8,0},{1,9},{9,1},{2,10},{10,2},{3,11},{11,3},{4,12},{12,4},... | collective-permute-start | bytes 4325384 | tf_op jit(solution)/shard_map/ppermute | solution.py:573
  (60 other events, 85.0 us)
where the time goes:
time: 310 us; the launch traced here: 304 us
  waiting for transfers between devices  99.6 us (32%)
  starting transfers between devices  71.8 us (23%)
  local copies, waits for them, and re-layouts  49.9 us (16%)
  other arithmetic  34.9 us (11%)
  matrix products  27.7 us (9%)
  Pallas kernels  17.2 us (6%)
    all_to_all x2, waiting for transfers between devices, exchange(): whole = lax.all_to_all(mine, ROW_AXES, 0, 0, tiled=True)  39.2 us
    dot_general x22, matrix products, take_rows(): return jnp.dot(choice, rows, preferred_element_type=f32).astype(bf16)  21.2 us
    all_to_all x2, waiting for transfers between devices, broadcast_all(): lax.all_to_all(jnp.broadcast_to(piece[None], (count,) + piece.shape), axe...  17.4 us
    unnamed x225, local copies, waits for them, and re-layouts  14.9 us
    all_to_all x2, waiting for transfers between devices, exchange(): lax.all_to_all(sent, COLUMN_AXES, 0, 0, tiled=True).reshape(-1, channels)  14.6 us
    all_to_all x2, waiting for transfers between devices, exchange(): lax.all_to_all(spread, 'z', 0, 0, tiled=True).reshape(Z * piece, channels)  14.5 us
    all_to_all x2, starting transfers between devices, exchange(): lax.all_to_all(sent, COLUMN_AXES, 0, 0, tiled=True).reshape(-1, channels)  14.1 us
    all_to_all x2, starting transfers between devices, exchange(): lax.all_to_all(spread, 'z', 0, 0, tiled=True).reshape(Z * piece, channels)  12.8 us
  transfers between devices with their start and end apart: 15, of which 11 were waited for; matrix products, arithmetic and copies ran while one was open for 13% of the time, Pallas kernels for 3%

commit v1 on v0

--- a/solution.py
+++ b/solution.py
@@ -30,7 +30,7 @@
     return (group // (Z * CORE)) * CORE + group % CORE
 
 
-def routing(matching, strip, channels):
+def routing(matching, strip):
     tiles = matching.shape[0]
     here = tiles // (XH * Z * CORE)
     lines = here * 4
@@ -83,10 +83,6 @@
     def places(position, step, base):
         return (position * step + line * base).reshape(-1)
 
-    kind = jnp.broadcast_to(mine[:, 1:2], (lines, width)).reshape(-1)
-    kind = (kind[None, :, None] == np.arange(4, dtype=np.int32)[:, None, None]).astype(bf16)
-    kind = jnp.broadcast_to(kind, (4, count, channels))
-    ends = jnp.repeat(own(finish).T, 2, axis=0)
     turned = jnp.where(
         flipped, places(width - 1 - position, lines, 1), places(position, lines, 1)
     )
@@ -99,10 +95,9 @@
         "flip": rows_of(flip, count),
         "flipped": flipped,
         "side": mine[:, 1],
-        "kind": kind,
-        "corner": rows_of(ends.reshape(-1) * (4 * lines) + np.arange(4 * lines, dtype=np.int32), 8 * lines),
         "quarter": mine[:, 3],
         "quarter_corner": my_corners[..., 3].T,
+        "finish": own(finish).T == 1,
         "row": row,
     }
 
@@ -204,12 +199,13 @@
     return spread, take_rows(rows_of(order[: piece // UNITS], piece), held)
 
 
-def exchange(spread, first_own, tiles, plan, rider=None):
+def exchange(spread, first_own, tiles, plan, rider=None, later=()):
     lines = tiles * 4
     line, channels = first_own.shape
     piece = UNITS * line
     width = ROWS * line // lines
     gathered = lax.all_to_all(spread, "z", 0, 0, tiled=True).reshape(Z * piece, channels)
+    gathered, later = lax.optimization_barrier((gathered, later))
     sent = take_rows(plan["pick"], gathered).reshape(XH * CORE, -1, channels)
     arrived = lax.all_to_all(sent, COLUMN_AXES, 0, 0, tiled=True).reshape(-1, channels)
     mine = jnp.concatenate([take_rows(plan["select"], arrived), first_own], axis=0)
@@ -221,8 +217,8 @@
     first = whole[:, :line].reshape(ROWS * line, channels)
     second = whole[:, line : 2 * line].reshape(ROWS * line, channels)
     own = whole[:, piece + 4 * lines : count].reshape(ROWS * line, channels)
-    corner = whole[:: ROWS - 1, piece : piece + 4 * lines].reshape(8 * lines, channels)
-    corner = take_rows(plan["corner"], corner).reshape(2, 2, lines, channels)
+    corner = whole[:, piece : piece + 4 * lines].reshape(ROWS, 2, 2, lines, channels)
+    corner = jnp.where(plan["finish"][:, None, :, None], corner[ROWS - 1], corner[0])
     corner = turn_channels(corner, plan["quarter_corner"][:, None])
     return (
         to_here(first, plan, "turned"),
@@ -231,6 +227,7 @@
         to_neighbour(own, plan, "turned"),
         corner,
         whole[:, count:],
+        later,
     )
 
 
@@ -242,7 +239,7 @@
     return jnp.concatenate(blocks, axis=-1)
 
 
-def edge_terms(patch_ref, kind_ref, weight_ref, out_ref, cells_ref):
+def edge_terms(patch_ref, side_ref, weight_ref, out_ref, cells_ref, kind_ref):
     depths, lines = patch_ref.shape[:2]
     width = patch_ref.shape[2] - 2
     for depth in range(depths):
@@ -250,6 +247,10 @@
             cells = patch_ref[depth, line]
             for tap in range(3):
                 cells_ref[depth * 3 + tap, line * width : (line + 1) * width] = shifted(cells, tap)
+    for line in range(lines):
+        for side in range(4):
+            kind = jnp.full((width, kind_ref.shape[2]), side_ref[line] == side, f32)
+            kind_ref[side, line * width : (line + 1) * width] = kind.astype(bf16)
     part = lines * width // 2
     for half in range(2):
         total = None
@@ -279,12 +280,15 @@
     total = pl.pallas_call(
         edge_terms,
         out_shape=jax.ShapeDtypeStruct((lines * width, channels), f32),
-        in_specs=[WHOLE] * 3,
+        in_specs=[WHOLE, pl.BlockSpec(memory_space=pltpu.SMEM), WHOLE],
         out_specs=WHOLE,
-        scratch_shapes=[pltpu.VMEM((9, lines * width, channels), bf16)],
+        scratch_shapes=[
+            pltpu.VMEM((9, lines * width, channels), bf16),
+            pltpu.VMEM((4, lines * width, channels), bf16),
+        ],
         compiler_params=ROOM,
         cost_estimate=CHEAP,
-    )(patch, plan["kind"], kernel_weight)
+    )(patch, plan["side"], kernel_weight)
     return total.reshape(lines, width, channels), patch
 
 
@@ -592,11 +596,11 @@
 
     ends, sides = outer_lines(activations, 0, lax.axis_index(ROW_AXES))
     pieces, first_own = offer(share_ends(ends), sides, tiles)
-    pieces, first_rows, last_rows, matching = lax.optimization_barrier(
-        (pieces, first_rows, last_rows, matching)
-    )
-    plan = routing(matching, strip, channels)
-    ghosts, edge, inner, own, corner, _ = exchange(pieces, first_own, tiles, plan)
+    pieces, matching = lax.optimization_barrier((pieces, matching))
+    plan = routing(matching, strip)
+    ghosts, edge, inner, own, corner, _, (first_rows, last_rows) = exchange(
+        pieces, first_own, tiles, plan, None, (first_rows, last_rows)
+    )
     above = lax.ppermute(last_rows, ROW_AXES, [(i, i + 1) for i in range(ROWS - 1)])
     below = lax.ppermute(first_rows, ROW_AXES, [(i + 1, i) for i in range(ROWS - 1)])
     cells = 4 * width
@@ -647,7 +651,7 @@
         ]
     )
 
-    routed, _, inner, own, corner, parts = exchange(
+    routed, _, inner, own, corner, parts, _ = exchange(
         pieces, first_own, tiles, plan, parts
     )
     routed = sides_of(routed)

time: 310 us -> 307 us (level)
    all_to_all x2, waiting for transfers between devices: 14.6 us -> 8.63 us  [exchange(): lax.all_to_all(sent, COLUMN_AXES, 0, 0, tiled=True).reshape(-1, channels)]
    all_to_all x2, waiting for transfers between devices: 14.5 us -> 18.5 us  [exchange(): lax.all_to_all(spread, 'z', 0, 0, tiled=True).reshape(Z * piece, channels)]
    dot_general x22 -> x20, matrix products: 21.2 us -> 19.4 us  [take_rows(): return jnp.dot(choice, rows, preferred_element_type=f32).astype(bf16)]
    unnamed x225 -> x217, local copies, waits for them, and re-layouts: 14.9 us -> 15.2 us
where the time goes in v1:
time: 307 us; the launch traced here: 301 us
  waiting for transfers between devices  101 us (33%)
  starting transfers between devices  69.4 us (23%)
  local copies, waits for them, and re-layouts  49.4 us (16%)
  other arithmetic  35.2 us (11%)
  matrix products  25.9 us (8%)
  Pallas kernels  17.7 us (6%)
    all_to_all x2, waiting for transfers between devices, exchange(): whole = lax.all_to_all(mine, ROW_AXES, 0, 0, tiled=True)  42.2 us
    dot_general x20, matrix products, take_rows(): return jnp.dot(choice, rows, preferred_element_type=f32).astype(bf16)  19.4 us
    all_to_all x2, waiting for transfers between devices, exchange(): lax.all_to_all(spread, 'z', 0, 0, tiled=True).reshape(Z * piece, channels)  18.5 us
    all_to_all x2, waiting for transfers between devices, broadcast_all(): lax.all_to_all(jnp.broadcast_to(piece[None], (count,) + piece.shape), axe...  17.4 us
    unnamed x217, local copies, waits for them, and re-layouts  15.2 us
    all_to_all x2, starting transfers between devices, exchange(): lax.all_to_all(sent, COLUMN_AXES, 0, 0, tiled=True).reshape(-1, channels)  13.7 us
    all_to_all x2, starting transfers between devices, exchange(): lax.all_to_all(spread, 'z', 0, 0, tiled=True).reshape(Z * piece, channels)  12.8 us
    all_to_all x2, starting transfers between devices, share_ends(): return lax.all_to_all(ends, ROW_AXES, 0, 0, tiled=True)  9.95 us
  transfers between devices with their start and end apart: 15, of which 11 were waited for; matrix products, arithmetic and copies ran while one was open for 13% of the time, Pallas kernels for 3%

profile of v1, /device:TPU:1, one launch (start us, length us, event | category | flops | bytes accessed | tf_op | source)
XLA Modules:
  0.0 301.0 jit_solution(6016513177822327367)
XLA Ops:
  1.4 1.5 fusion.38
  3.6 5.9 %all-to-all-start = ((bf16[8,36,256]{2,1,0:T(8,128)(2,1)}), bf16[8,36,256]{2,1,0:T(8,128)(2,1)S(1)}, u32[]{:S(2)}, u32[]{:S(2)}) async-start(bf16[8,36,256]{2,1,0:T(8,128)(2,1)} %reshape.705), calls=%async_computation | async-start | bytes 327680 | tf_op jit(solution)/shard_map/all_to_all | solution.py:185
  10.4 4.9 %all-to-all-done = bf16[8,36,256]{2,1,0:T(8,128)(2,1)S(1)} async-done(((bf16[8,36,256]{2,1,0:T(8,128)(2,1)}), bf16[8,36,256]{2,1,0:T(8,128)(2,1)S(1)}, u32[]{:S(2)}, u32[]{:S(2)}) %all-to-all-start) | async-done | bytes 147488 | tf_op jit(solution)/shard_map/all_to_all | solution.py:185
  15.3 1.2 convolution_convert_fusion.1
  18.9 8.2 %all-to-all-start.1 = ((bf16[8,144,256]{2,1,0:T(8,128)(2,1)}), bf16[8,144,256]{2,1,0:T(8,128)(2,1)S(1)}, u32[]{:S(2)}, u32[]{:S(2)}) async-start(bf16[8,144,256]{2,1,0:T(8,128)(2,1)} %bitcast.3), calls=%async_computation.1 | async-start | bytes 1179648 | tf_op jit(solution)/shard_map/all_to_all | solution.py:207
  32.0 12.0 %all-to-all-done.1 = bf16[8,144,256]{2,1,0:T(8,128)(2,1)S(1)} async-done(((bf16[8,144,256]{2,1,0:T(8,128)(2,1)}), bf16[8,144,256]{2,1,0:T(8,128)(2,1)S(1)}, u32[]{:S(2)}, u32[]{:S(2)}) %all-to-all-start.1) | async-done | bytes 589856 | tf_op jit(solution)/shard_map/all_to_all | solution.py:207
  44.1 1.5 fusion.17
  45.6 6.9 %all-to-all-start.2 = ((bf16[4,192,256]{2,1,0:T(8,128)(2,1)}), bf16[4,192,256]{2,1,0:T(8,128)(2,1)S(1)}, u32[]{:S(2)}, u32[]{:S(2)}) async-start(bf16[4,192,256]{2,1,0:T(8,128)(2,1)} %bitcast.43), calls=%async_computation.2 | async-start | bytes 786432 | tf_op jit(solution)/shard_map/all_to_all | solution.py:210
  53.3 1.3 collective-permute-start.1
  54.6 4.0 %collective-permute-start = (bf16[3,216,256]{2,1,0:T(8,128)(2,1)S(1)}, bf16[3,216,256]{2,1,0:T(8,128)(2,1)S(1)}, u32[]{:S(2)}, u32[]{:S(2)}) collective-permute-start(bf16[3,216,256]{2,1,0:T(8,128)(2,1)S(1)} %get-tuple-element.20), channel_id=1, source_target_pairs={{0,1},{1,2},{2,3},{3,4},{4,5},{5,6},{6,7},{8,9},{9,10},{10,11},{11... | collective-permute-start | bytes 995336 | tf_op jit(solution)/shard_map/ppermute | solution.py:604
  58.6 2.0 all-to-all-done.2
  62.0 4.4 %all-to-all-start.3 = ((bf16[8,264,256]{2,1,0:T(8,128)(2,1)}), bf16[8,264,256]{2,1,0:T(8,128)(2,1)}, u32[]{:S(2)}, u32[]{:S(2)}) async-start(bf16[8,264,256]{2,1,0:T(8,128)(2,1)} %broadcast_in_dim.562), calls=%async_computation.3 | async-start | bytes 2162688 | tf_op jit(solution)/shard_map/all_to_all | solution.py:216
  70.0 15.1 %all-to-all-done.3 = bf16[8,264,256]{2,1,0:T(8,128)(2,1)} async-done(((bf16[8,264,256]{2,1,0:T(8,128)(2,1)}), bf16[8,264,256]{2,1,0:T(8,128)(2,1)}, u32[]{:S(2)}, u32[]{:S(2)}) %all-to-all-start.3) | async-done | bytes 1081376 | tf_op jit(solution)/shard_map/all_to_all | solution.py:216
  85.1 1.2 fusion.167
  86.7 1.2 fusion.23
  91.5 3.4 %shard_map.299 = f32[576,256]{1,0:T(8,128)S(1)} custom-call(bf16[3,12,50,256]{3,2,1,0:T(8,128)(2,1)S(1)} %pad_maximum_fusion.7.patch_ref, s32[12]{0:T(128)S(1)} %slice_bitcast_fusion.34.side_ref, bf16[3,3,256,256]{3,2,1,0:T(8,128)(2,1)S(1)} %copy-done.3), custom_call_target="tpu_custom_call" | custom-call | flops 1000 | bytes 1000 | tf_op jit(solution)/shard_map/pallas_call | solution.py:280
  98.2 1.7 pad_maximum_fusion.5.padded_ref
  99.9 2.1 reshape.715
  102.1 1.3 copy-done.11
  103.3 2.2 shard_map.300
  108.1 1.9 shard_map.301
  111.1 1.4 pad.41.padded_ref
  113.3 1.3 copy-done.19
  114.6 1.2 copy-done.20
  115.8 2.0 shard_map.302
  120.2 1.4 add_multiply_fusion
  125.0 4.0 %all-to-all-start.4 = ((bf16[8,36,256]{2,1,0:T(8,128)(2,1)}), bf16[8,36,256]{2,1,0:T(8,128)(2,1)}, u32[]{:S(2)}, u32[]{:S(2)}) async-start(bf16[8,36,256]{2,1,0:T(8,128)(2,1)} %reshape.732), calls=%async_computation.4 | async-start | bytes 327680 | tf_op jit(solution)/shard_map/all_to_all | solution.py:185
  131.1 1.4 shard_map.304
  133.5 1.9 reshape.741
  135.5 1.8 copy.134
  138.7 2.0 convolution_convert_fusion
  140.7 4.6 %all-to-all-start.5 = ((bf16[8,144,256]{2,1,0:T(8,128)(2,1)}), bf16[8,144,256]{2,1,0:T(8,128)(2,1)}, u32[]{:S(2)}, u32[]{:S(2)}) async-start(bf16[8,144,256]{2,1,0:T(8,128)(2,1)} %bitcast.342), calls=%async_computation.5 | async-start | bytes 1179648 | tf_op jit(solution)/shard_map/all_to_all | solution.py:207
  145.3 2.0 fusion.29
  150.6 5.1 %shard_map.303 = f32[9,256,256]{2,1,0:T(8,128)S(1)} custom-call(bf16[3,8,50,256]{3,2,1,0:T(8,128)(2,1)S(1)} %copy-done.24, bf16[3,6,48,256]{3,2,1,0:T(8,128)(2,1)S(1)} %fusion.42.grads_ref, bf16[3,12,50,256]{3,2,1,0:T(8,128)(2,1)S(1)} %copy-done.10, bf16[576,1024]{1,0:T(8,128)(2,1)S(1)} %pad_maximum_fusion.6.edge_ref), custom_call_target="tpu_custom_call" | custom-call | flops 1000 | bytes 1000 | tf_op jit(solution)/shard_map/pallas_call | solution.py:471
  155.7 1.7 select_convert_fusion
  158.1 6.6 %all-to-all-done.5 = bf16[8,144,256]{2,1,0:T(8,128)(2,1)} async-done(((bf16[8,144,256]{2,1,0:T(8,128)(2,1)}), bf16[8,144,256]{2,1,0:T(8,128)(2,1)}, u32[]{:S(2)}, u32[]{:S(2)}) %all-to-all-start.5) | async-done | bytes 589856 | tf_op jit(solution)/shard_map/all_to_all | solution.py:207
  164.7 2.6 fusion.18
  167.2 6.8 %all-to-all-start.6 = ((bf16[4,192,256]{2,1,0:T(8,128)(2,1)}), bf16[4,192,256]{2,1,0:T(8,128)(2,1)}, u32[]{:S(2)}, u32[]{:S(2)}) async-start(bf16[4,192,256]{2,1,0:T(8,128)(2,1)} %bitcast.344), calls=%async_computation.6 | async-start | bytes 786432 | tf_op jit(solution)/shard_map/all_to_all | solution.py:210
  174.0 1.6 convolution_convert_fusion.4
  175.6 6.6 %all-to-all-done.6 = bf16[4,192,256]{2,1,0:T(8,128)(2,1)} async-done(((bf16[4,192,256]{2,1,0:T(8,128)(2,1)}), bf16[4,192,256]{2,1,0:T(8,128)(2,1)}, u32[]{:S(2)}, u32[]{:S(2)}) %all-to-all-start.6) | async-done | bytes 393248 | tf_op jit(solution)/shard_map/all_to_all | solution.py:210
  182.2 1.3 convolution_convert_fusion.2
  184.3 2.9 add_convert_fusion
  187.3 1.7 pad_maximum_fusion.2
  188.9 4.6 %all-to-all-start.7 = ((bf16[8,616,256]{2,1,0:T(8,128)(2,1)}), bf16[8,616,256]{2,1,0:T(8,128)(2,1)}, u32[]{:S(2)}, u32[]{:S(2)}) async-start(bf16[8,616,256]{2,1,0:T(8,128)(2,1)} %pad_maximum_fusion.2), calls=%async_computation.7 | async-start | bytes 5046272 | tf_op jit(solution)/shard_map/all_to_all | solution.py:216
  197.0 27.1 %all-to-all-done.7 = bf16[8,616,256]{2,1,0:T(8,128)(2,1)} async-done(((bf16[8,616,256]{2,1,0:T(8,128)(2,1)}), bf16[8,616,256]{2,1,0:T(8,128)(2,1)}, u32[]{:S(2)}, u32[]{:S(2)}) %all-to-all-start.7) | async-done | bytes 2523168 | tf_op jit(solution)/shard_map/all_to_all | solution.py:216
  225.0 1.2 fusion.166
  232.6 1.6 slice_reduce_fusion
  234.9 4.3 %all-to-all-start.8 = ((bf16[16,22,256]{2,1,0:T(8,128)(2,1)}), bf16[16,22,256]{2,1,0:T(8,128)(2,1)}, u32[]{:S(2)}, u32[]{:S(2)}) async-start(bf16[16,22,256]{2,1,0:T(8,128)(2,1)} %reshape.746), calls=%async_computation.8 | async-start | bytes 393216 | tf_op jit(solution)/shard_map/all_to_all | solution.py:567
  239.3 1.8 slice_bitcast_fusion.5
  242.3 6.0 %all-to-all-done.8 = bf16[16,22,256]{2,1,0:T(8,128)(2,1)} async-done(((bf16[16,22,256]{2,1,0:T(8,128)(2,1)}), bf16[16,22,256]{2,1,0:T(8,128)(2,1)}, u32[]{:S(2)}, u32[]{:S(2)}) %all-to-all-start.8) | async-done | bytes 180256 | tf_op jit(solution)/shard_map/all_to_all | solution.py:567
  250.0 4.2 %all-to-all-start.9 = ((bf16[16,22,256]{2,1,0:T(8,128)(2,1)}), bf16[16,22,256]{2,1,0:T(8,128)(2,1)}, u32[]{:S(2)}, u32[]{:S(2)}) async-start(bf16[16,22,256]{2,1,0:T(8,128)(2,1)} %broadcast_in_dim.590), calls=%async_computation.9 | async-start | bytes 393216 | tf_op jit(solution)/shard_map/all_to_all | solution.py:24
  254.2 2.4 fusion.61
  256.9 1.1 convolution_add_fusion.3
  258.0 1.2 shard_map.306
  259.3 3.9 %all-to-all-done.9 = bf16[16,22,256]{2,1,0:T(8,128)(2,1)} async-done(((bf16[16,22,256]{2,1,0:T(8,128)(2,1)}), bf16[16,22,256]{2,1,0:T(8,128)(2,1)}, u32[]{:S(2)}, u32[]{:S(2)}) %all-to-all-start.9) | async-done | bytes 180256 | tf_op jit(solution)/shard_map/all_to_all | solution.py:24
  264.1 1.2 broadcast_in_dim.604
  265.3 5.7 %all-to-all-start.10 = ((bf16[8,352,256]{2,1,0:T(8,128)(2,1)}), bf16[8,352,256]{2,1,0:T(8,128)(2,1)}, u32[]{:S(2)}, u32[]{:S(2)}) async-start(bf16[8,352,256]{2,1,0:T(8,128)(2,1)} %broadcast_in_dim.604), calls=%async_computation.10 | async-start | bytes 2883584 | tf_op jit(solution)/shard_map/all_to_all | solution.py:24
  271.0 1.7 fusion.40
  273.4 1.1 add_convert_fusion.1
  274.5 13.5 %all-to-all-done.10 = bf16[8,352,256]{2,1,0:T(8,128)(2,1)} async-done(((bf16[8,352,256]{2,1,0:T(8,128)(2,1)}), bf16[8,352,256]{2,1,0:T(8,128)(2,1)}, u32[]{:S(2)}, u32[]{:S(2)}) %all-to-all-start.10) | async-done | bytes 1441824 | tf_op jit(solution)/shard_map/all_to_all | solution.py:24
  288.0 4.0 %collective-permute-start.3 = (bf16[2816,256]{1,0:T(8,128)(2,1)}, bf16[2816,256]{1,0:T(8,128)(2,1)S(1)}, u32[]{:S(2)}, u32[]{:S(2)}) collective-permute-start(bf16[2816,256]{1,0:T(8,128)(2,1)} %bitcast.105), channel_id=1, source_target_pairs={{0,8},{8,0},{1,9},{9,1},{2,10},{10,2},{3,11},{11,3},{4,12},{12,4},... | collective-permute-start | bytes 4325384 | tf_op jit(solution)/shard_map/ppermute | solution.py:577
  292.0 3.1 %collective-permute-done.3 = bf16[2816,256]{1,0:T(8,128)(2,1)S(1)} collective-permute-done((bf16[2816,256]{1,0:T(8,128)(2,1)}, bf16[2816,256]{1,0:T(8,128)(2,1)S(1)}, u32[]{:S(2)}, u32[]{:S(2)}) %collective-permute-start.3) | collective-permute-done | bytes 1441824 | tf_op jit(solution)/shard_map/ppermute | solution.py:577
  295.1 1.7 broadcast_select_fusion.1
  298.3 2.5 fusion.164
  (406 shorter events, 58.4 us)
Async XLA Ops:
  0.6 8.9 %copy-start.32 = (bf16[3,6,48,256]{3,2,1,0:T(8,128)(2,1)S(1)}, bf16[3,6,48,256]{3,2,1,0:T(8,128)(2,1)}, u32[]{:S(2)}) copy-start(bf16[3,6,48,256]{3,2,1,0:T(8,128)(2,1)} %param.28) | copy-start | bytes 1327108
  1.4 8.3 %copy-start.26 = (bf16[3,3,24,256]{3,2,1,0:T(8,128)(2,1)S(1)}, bf16[3,3,24,256]{3,2,1,0:T(8,128)(2,1)}, u32[]{:S(2)}) copy-start(bf16[3,3,24,256]{3,2,1,0:T(8,128)(2,1)} %param.33) | copy-start | bytes 331780
  1.4 8.3 %copy-start.95 = (s32[360]{0:T(512)S(1)}, s32[360]{0:T(512)}, u32[]{:S(2)}) copy-start(s32[360]{0:T(512)} %constant.350.clone) | copy-start | bytes 4324
  1.4 8.3 %copy-start.96 = (s32[360]{0:T(512)S(1)}, s32[360]{0:T(512)}, u32[]{:S(2)}) copy-start(s32[360]{0:T(512)} %constant.351.clone) | copy-start | bytes 4324
  2.9 7.4 %copy-start.100 = (s32[4]{0:T(128)S(1)}, s32[4]{0:T(128)}, u32[]{:S(2)}) copy-start(s32[4]{0:T(128)} %constant.344.clone) | copy-start | bytes 52
  2.9 7.4 %copy-start.101 = (s32[4]{0:T(128)S(1)}, s32[4]{0:T(128)}, u32[]{:S(2)}) copy-start(s32[4]{0:T(128)} %constant.345.clone) | copy-start | bytes 52
  3.6 11.7 %all-to-all-start = ((bf16[8,36,256]{2,1,0:T(8,128)(2,1)}), bf16[8,36,256]{2,1,0:T(8,128)(2,1)S(1)}, u32[]{:S(2)}, u32[]{:S(2)}) async-start(bf16[8,36,256]{2,1,0:T(8,128)(2,1)} %reshape.705), calls=%async_computation | async-start | bytes 327680 | tf_op jit(solution)/shard_map/all_to_all | solution.py:185
  9.6 5.7 %copy-start.102 = (s32[1152]{0:T(1024)S(1)}, s32[1152]{0:T(1024)}, u32[]{:S(2)}) copy-start(s32[1152]{0:T(1024)} %constant.379) | copy-start | bytes 13828
  9.6 6.8 %copy-start.44 = (s32[96,4,4]{0,2,1:T(4,128)S(1)}, s32[96,4,4]{0,2,1:T(4,128)}, u32[]{:S(2)}) copy-start(s32[96,4,4]{0,2,1:T(4,128)} %param.29) | copy-start | bytes 18436
  16.8 15.1 %copy-start.103 = (s32[72]{0:T(128)S(1)}, s32[72]{0:T(128)}, u32[]{:S(2)}) copy-start(s32[72]{0:T(128)} %constant.381) | copy-start | bytes 868
  18.9 26.7 %copy-start.55 = (pred[12]{0:T(512)(128)(4,1)}, pred[12]{0:T(512)(128)(4,1)S(1)}, u32[]{:S(2)}) copy-start(pred[12]{0:T(512)(128)(4,1)S(1)} %get-tuple-element.118) | copy-start | bytes 40
  18.9 26.7 %copy-start.57 = (pred[12]{0:T(512)(128)(4,1)}, pred[12]{0:T(512)(128)(4,1)S(1)}, u32[]{:S(2)}) copy-start(pred[12]{0:T(512)(128)(4,1)S(1)} %get-tuple-element.119) | copy-start | bytes 40
  18.9 26.7 %copy-start.59 = (pred[12]{0:T(512)(128)(4,1)}, pred[12]{0:T(512)(128)(4,1)S(1)}, u32[]{:S(2)}) copy-start(pred[12]{0:T(512)(128)(4,1)S(1)} %get-tuple-element.120) | copy-start | bytes 40
  18.9 25.1 %all-to-all-start.1 = ((bf16[8,144,256]{2,1,0:T(8,128)(2,1)}), bf16[8,144,256]{2,1,0:T(8,128)(2,1)S(1)}, u32[]{:S(2)}, u32[]{:S(2)}) async-start(bf16[8,144,256]{2,1,0:T(8,128)(2,1)} %bitcast.3), calls=%async_computation.1 | async-start | bytes 1179648 | tf_op jit(solution)/shard_map/all_to_all | solution.py:207
  28.2 17.4 %copy-start.78 = (s32[768]{0:T(1024)}, s32[768]{0:T(1024)S(1)}, u32[]{:S(2)}) copy-start(s32[768]{0:T(1024)S(1)} %eq.488) | copy-start | bytes 9220
  28.6 32.1 %copy-start.97 = (s32[192]{0:T(256)}, s32[192]{0:T(256)S(1)}, u32[]{:S(2)}) copy-start(s32[192]{0:T(256)S(1)} %iota_add_fusion) | copy-start | bytes 2308
  31.8 57.4 %copy-start.63 = (pred[2,12]{1,0:T(4,128)(4,1)}, pred[2,12]{1,0:T(4,128)(4,1)S(1)}, u32[]{:S(2)}) copy-start(pred[2,12]{1,0:T(4,128)(4,1)S(1)} %get-tuple-element.137) | copy-start | bytes 76
  31.8 57.4 %copy-start.65 = (pred[2,12]{1,0:T(4,128)(4,1)}, pred[2,12]{1,0:T(4,128)(4,1)S(1)}, u32[]{:S(2)}) copy-start(pred[2,12]{1,0:T(4,128)(4,1)S(1)} %get-tuple-element.138) | copy-start | bytes 76
  31.8 57.4 %copy-start.67 = (pred[2,12]{1,0:T(4,128)(4,1)}, pred[2,12]{1,0:T(4,128)(4,1)S(1)}, u32[]{:S(2)}) copy-start(pred[2,12]{1,0:T(4,128)(4,1)S(1)} %get-tuple-element.139) | copy-start | bytes 76
  44.0 8.6 %copy-start.72 = (s32[576]{0:T(1024)S(1)}, s32[576]{0:T(1024)}, u32[]{:S(2)}) copy-start(s32[576]{0:T(1024)} %constant.347.clone) | copy-start | bytes 6916
  44.0 8.6 %copy-start.80 = (s32[576]{0:T(1024)S(1)}, s32[576]{0:T(1024)}, u32[]{:S(2)}) copy-start(s32[576]{0:T(1024)} %constant.346.clone) | copy-start | bytes 6916
  44.0 8.6 %copy-start.81 = (s32[576]{0:T(1024)S(1)}, s32[576]{0:T(1024)}, u32[]{:S(2)}) copy-start(s32[576]{0:T(1024)} %constant.348.clone) | copy-start | bytes 6916
  44.0 8.6 %copy-start.82 = (s32[576]{0:T(1024)S(1)}, s32[576]{0:T(1024)}, u32[]{:S(2)}) copy-start(s32[576]{0:T(1024)} %constant.352.clone) | copy-start | bytes 6916
  44.0 8.6 %copy-start.83 = (s32[576]{0:T(1024)S(1)}, s32[576]{0:T(1024)}, u32[]{:S(2)}) copy-start(s32[576]{0:T(1024)} %constant.353.clone) | copy-start | bytes 6916
  44.0 8.6 %copy-start.84 = (s32[576]{0:T(1024)S(1)}, s32[576]{0:T(1024)}, u32[]{:S(2)}) copy-start(s32[576]{0:T(1024)} %constant.354.clone) | copy-start | bytes 6916
  44.0 8.6 %copy-start.85 = (s32[576]{0:T(1024)S(1)}, s32[576]{0:T(1024)}, u32[]{:S(2)}) copy-start(s32[576]{0:T(1024)} %constant.355.clone) | copy-start | bytes 6916
  44.1 8.6 %copy-start.86 = (s32[576]{0:T(1024)S(1)}, s32[576]{0:T(1024)}, u32[]{:S(2)}) copy-start(s32[576]{0:T(1024)} %constant.356.clone) | copy-start | bytes 6916
  45.6 15.0 %all-to-all-start.2 = ((bf16[4,192,256]{2,1,0:T(8,128)(2,1)}), bf16[4,192,256]{2,1,0:T(8,128)(2,1)S(1)}, u32[]{:S(2)}, u32[]{:S(2)}) async-start(bf16[4,192,256]{2,1,0:T(8,128)(2,1)} %bitcast.43), calls=%async_computation.2 | async-start | bytes 786432 | tf_op jit(solution)/shard_map/all_to_all | solution.py:210
  52.7 36.4 %copy-start.69 = (pred[2,12]{1,0:T(4,128)(4,1)}, pred[2,12]{1,0:T(4,128)(4,1)S(1)}, u32[]{:S(2)}) copy-start(pred[2,12]{1,0:T(4,128)(4,1)S(1)} %compare_bitcast_fusion) | copy-start | bytes 76
  53.3 34.6 %copy-start.74 = (s32[576]{0:T(1024)}, s32[576]{0:T(1024)S(1)}, u32[]{:S(2)}) copy-start(s32[576]{0:T(1024)S(1)} %get-tuple-element.135) | copy-start | bytes 6916
  53.3 41.7 %copy-start.76 = (s32[576]{0:T(1024)}, s32[576]{0:T(1024)S(1)}, u32[]{:S(2)}) copy-start(s32[576]{0:T(1024)S(1)} %get-tuple-element.136) | copy-start | bytes 6916
  53.3 13.2 %collective-permute-start.1 = (bf16[3,216,256]{2,1,0:T(8,128)(2,1)S(1)}, bf16[3,216,256]{2,1,0:T(8,128)(2,1)S(1)}, u32[]{:S(2)}, u32[]{:S(2)}) collective-permute-start(bf16[3,216,256]{2,1,0:T(8,128)(2,1)S(1)} %get-tuple-element.21), channel_id=1, source_target_pairs={{1,0},{2,1},{3,2},{4,3},{5,4},{6,5},{7,6},{9,8},{10,9},{11,10},{12... | collective-permute-start | bytes 995336 | tf_op jit(solution)/shard_map/ppermute | solution.py:605
  54.6 11.9 %collective-permute-start = (bf16[3,216,256]{2,1,0:T(8,128)(2,1)S(1)}, bf16[3,216,256]{2,1,0:T(8,128)(2,1)S(1)}, u32[]{:S(2)}, u32[]{:S(2)}) collective-permute-start(bf16[3,216,256]{2,1,0:T(8,128)(2,1)S(1)} %get-tuple-element.20), channel_id=1, source_target_pairs={{0,1},{1,2},{2,3},{3,4},{4,5},{5,6},{6,7},{8,9},{9,10},{10,11},{11... | collective-permute-start | bytes 995336 | tf_op jit(solution)/shard_map/ppermute | solution.py:604
  61.0 5.5 %copy-start.41 = (bf16[2,2,256,256]{3,2,1,0:T(8,128)(2,1)S(1)}, bf16[2,2,256,256]{3,2,1,0:T(8,128)(2,1)}, u32[]{:S(2)}) copy-start(bf16[2,2,256,256]{3,2,1,0:T(8,128)(2,1)} %param.32) | copy-start | bytes 1572868
  62.0 23.1 %all-to-all-start.3 = ((bf16[8,264,256]{2,1,0:T(8,128)(2,1)}), bf16[8,264,256]{2,1,0:T(8,128)(2,1)}, u32[]{:S(2)}, u32[]{:S(2)}) async-start(bf16[8,264,256]{2,1,0:T(8,128)(2,1)} %broadcast_in_dim.562), calls=%async_computation.3 | async-start | bytes 2162688 | tf_op jit(solution)/shard_map/all_to_all | solution.py:216
  91.5 4.0 %copy-start.9 = (bf16[3,12,50,256]{3,2,1,0:T(8,128)(2,1)}, bf16[3,12,50,256]{3,2,1,0:T(8,128)(2,1)S(1)}, u32[]{:S(2)}) copy-start(bf16[3,12,50,256]{3,2,1,0:T(8,128)(2,1)S(1)} %pad_maximum_fusion.7.patch_ref) | copy-start | bytes 2764804
  105.6 14.6 %copy-start.1 = (f32[3,12,48,256]{3,2,1,0:T(8,128)}, f32[3,12,48,256]{3,2,1,0:T(8,128)S(1)}, u32[]{:S(2)}) copy-start(f32[3,12,48,256]{3,2,1,0:T(8,128)S(1)} %shard_map.300) | copy-start | bytes 5308420
  119.6 3.0 copy-start.40
  125.0 12.4 %all-to-all-start.4 = ((bf16[8,36,256]{2,1,0:T(8,128)(2,1)}), bf16[8,36,256]{2,1,0:T(8,128)(2,1)}, u32[]{:S(2)}, u32[]{:S(2)}) async-start(bf16[8,36,256]{2,1,0:T(8,128)(2,1)} %reshape.732), calls=%async_computation.4 | async-start | bytes 327680 | tf_op jit(solution)/shard_map/all_to_all | solution.py:185
  135.5 9.8 %copy-start.87 = (s32[576]{0:T(1024)S(1)}, s32[576]{0:T(1024)}, u32[]{:S(2)}) copy-start(s32[576]{0:T(1024)} %get-tuple-element.134) | copy-start | bytes 6916
  138.1 2.6 copy-start.46
  140.7 24.0 %all-to-all-start.5 = ((bf16[8,144,256]{2,1,0:T(8,128)(2,1)}), bf16[8,144,256]{2,1,0:T(8,128)(2,1)}, u32[]{:S(2)}, u32[]{:S(2)}) async-start(bf16[8,144,256]{2,1,0:T(8,128)(2,1)} %bitcast.342), calls=%async_computation.5 | async-start | bytes 1179648 | tf_op jit(solution)/shard_map/all_to_all | solution.py:207
  150.6 5.1 %copy-start.8 = (f32[4,256,256]{2,1,0:T(8,128)}, f32[4,256,256]{2,1,0:T(8,128)S(1)}, u32[]{:S(2)}) copy-start(f32[4,256,256]{2,1,0:T(8,128)S(1)} %shard_map.305) | copy-start | bytes 3145732
  155.7 8.9 %copy-start.79 = (s32[768]{0:T(1024)S(1)}, s32[768]{0:T(1024)}, u32[]{:S(2)}) copy-start(s32[768]{0:T(1024)} %copy-done.78) | copy-start | bytes 9220
  157.6 26.7 %collective-permute-start.2 = (bf16[2816,256]{1,0:T(8,128)(2,1)}, bf16[2816,256]{1,0:T(8,128)(2,1)}, u32[]{:S(2)}, u32[]{:S(2)}) collective-permute-start(bf16[2816,256]{1,0:T(8,128)(2,1)} %select_convert_fusion), channel_id=1, source_target_pairs={{0,8},{8,0},{1,9},{9,1},{2,10},{10,2},{3,11},{11,3},{4,12},{12,4},... | collective-permute-start | bytes 4325384 | tf_op jit(solution)/shard_map/ppermute | solution.py:559
  167.2 14.9 %all-to-all-start.6 = ((bf16[4,192,256]{2,1,0:T(8,128)(2,1)}), bf16[4,192,256]{2,1,0:T(8,128)(2,1)}, u32[]{:S(2)}, u32[]{:S(2)}) async-start(bf16[4,192,256]{2,1,0:T(8,128)(2,1)} %bitcast.344), calls=%async_computation.6 | async-start | bytes 786432 | tf_op jit(solution)/shard_map/all_to_all | solution.py:210
  188.9 35.1 %all-to-all-start.7 = ((bf16[8,616,256]{2,1,0:T(8,128)(2,1)}), bf16[8,616,256]{2,1,0:T(8,128)(2,1)}, u32[]{:S(2)}, u32[]{:S(2)}) async-start(bf16[8,616,256]{2,1,0:T(8,128)(2,1)} %pad_maximum_fusion.2), calls=%async_computation.7 | async-start | bytes 5046272 | tf_op jit(solution)/shard_map/all_to_all | solution.py:216
  195.2 32.1 %copy-start.47 = (pred[48]{0:T(512)(128)(4,1)}, pred[48]{0:T(512)(128)(4,1)S(1)}, u32[]{:S(2)}) copy-start(pred[48]{0:T(512)(128)(4,1)S(1)} %get-tuple-element.148) | copy-start | bytes 148
  195.8 29.0 %copy-start.70 = (pred[2,12]{1,0:T(4,128)(4,1)S(1)}, pred[2,12]{1,0:T(4,128)(4,1)}, u32[]{:S(2)}) copy-start(pred[2,12]{1,0:T(4,128)(4,1)} %copy-done.69) | copy-start | bytes 76
  195.8 29.1 %copy-start.64 = (pred[2,12]{1,0:T(4,128)(4,1)S(1)}, pred[2,12]{1,0:T(4,128)(4,1)}, u32[]{:S(2)}) copy-start(pred[2,12]{1,0:T(4,128)(4,1)} %copy-done.63) | copy-start | bytes 76
  195.8 29.1 %copy-start.66 = (pred[2,12]{1,0:T(4,128)(4,1)S(1)}, pred[2,12]{1,0:T(4,128)(4,1)}, u32[]{:S(2)}) copy-start(pred[2,12]{1,0:T(4,128)(4,1)} %copy-done.65) | copy-start | bytes 76
  195.8 29.1 %copy-start.68 = (pred[2,12]{1,0:T(4,128)(4,1)S(1)}, pred[2,12]{1,0:T(4,128)(4,1)}, u32[]{:S(2)}) copy-start(pred[2,12]{1,0:T(4,128)(4,1)} %copy-done.67) | copy-start | bytes 76
  196.1 30.2 %copy-start.75 = (s32[576]{0:T(1024)S(1)}, s32[576]{0:T(1024)}, u32[]{:S(2)}) copy-start(s32[576]{0:T(1024)} %copy-done.74) | copy-start | bytes 6916
  234.9 19.3 %copy-start.2 = (f32[3,12,48,256]{3,2,1,0:T(8,128)S(1)}, f32[3,12,48,256]{3,2,1,0:T(8,128)}, u32[]{:S(2)}) copy-start(f32[3,12,48,256]{3,2,1,0:T(8,128)} %copy-done.1) | copy-start | bytes 5308420
  234.9 19.3 %copy-start.48 = (pred[48]{0:T(512)(128)(4,1)S(1)}, pred[48]{0:T(512)(128)(4,1)}, u32[]{:S(2)}) copy-start(pred[48]{0:T(512)(128)(4,1)} %copy-done.47) | copy-start | bytes 148
  234.9 19.3 %copy-start.92 = (pred[8]{0:T(512)(128)(4,1)S(1)}, pred[8]{0:T(512)(128)(4,1)}, u32[]{:S(2)}) copy-start(pred[8]{0:T(512)(128)(4,1)} %get-tuple-element.149) | copy-start | bytes 28
  234.9 19.3 %copy-start.93 = (pred[8]{0:T(512)(128)(4,1)S(1)}, pred[8]{0:T(512)(128)(4,1)}, u32[]{:S(2)}) copy-start(pred[8]{0:T(512)(128)(4,1)} %get-tuple-element.150) | copy-start | bytes 28
  234.9 13.4 %all-to-all-start.8 = ((bf16[16,22,256]{2,1,0:T(8,128)(2,1)}), bf16[16,22,256]{2,1,0:T(8,128)(2,1)}, u32[]{:S(2)}, u32[]{:S(2)}) async-start(bf16[16,22,256]{2,1,0:T(8,128)(2,1)} %reshape.746), calls=%async_computation.8 | async-start | bytes 393216 | tf_op jit(solution)/shard_map/all_to_all | solution.py:567
  250.0 13.2 %all-to-all-start.9 = ((bf16[16,22,256]{2,1,0:T(8,128)(2,1)}), bf16[16,22,256]{2,1,0:T(8,128)(2,1)}, u32[]{:S(2)}, u32[]{:S(2)}) async-start(bf16[16,22,256]{2,1,0:T(8,128)(2,1)} %broadcast_in_dim.590), calls=%async_computation.9 | async-start | bytes 393216 | tf_op jit(solution)/shard_map/all_to_all | solution.py:24
  254.2 2.7 copy-start.35
  265.3 7.4 %copy-start.37 = (bf16[12,48,128]{2,1,0:T(8,128)(2,1)S(1)}, bf16[12,48,128]{2,1,0:T(8,128)(2,1)}, u32[]{:S(2)}) copy-start(bf16[12,48,128]{2,1,0:T(8,128)(2,1)} %get-tuple-element.132) | copy-start | bytes 442372
  265.3 7.4 %copy-start.38 = (bf16[12,48,128]{2,1,0:T(8,128)(2,1)S(1)}, bf16[12,48,128]{2,1,0:T(8,128)(2,1)}, u32[]{:S(2)}) copy-start(bf16[12,48,128]{2,1,0:T(8,128)(2,1)} %get-tuple-element.133) | copy-start | bytes 442372
  265.3 22.7 %all-to-all-start.10 = ((bf16[8,352,256]{2,1,0:T(8,128)(2,1)}), bf16[8,352,256]{2,1,0:T(8,128)(2,1)}, u32[]{:S(2)}, u32[]{:S(2)}) async-start(bf16[8,352,256]{2,1,0:T(8,128)(2,1)} %broadcast_in_dim.604), calls=%async_computation.10 | async-start | bytes 2883584 | tf_op jit(solution)/shard_map/all_to_all | solution.py:24
  288.0 7.1 %collective-permute-start.3 = (bf16[2816,256]{1,0:T(8,128)(2,1)}, bf16[2816,256]{1,0:T(8,128)(2,1)S(1)}, u32[]{:S(2)}, u32[]{:S(2)}) collective-permute-start(bf16[2816,256]{1,0:T(8,128)(2,1)} %bitcast.105), channel_id=1, source_target_pairs={{0,8},{8,0},{1,9},{9,1},{2,10},{10,2},{3,11},{11,3},{4,12},{12,4},... | collective-permute-start | bytes 4325384 | tf_op jit(solution)/shard_map/ppermute | solution.py:577
  (56 other events, 73.1 us)
